TPU v7x, 256 devices: a whole 4x4x8 slice. The times are simulated.
256 devices in a mesh: rows: 16 (over y_hi, z), cols: 4 (over y_lo, core), rep: 4 (over x).
Axes of the slice: x: 4, y: 4 (y_hi: 2, y_lo: 2; y = y_hi * 2 + y_lo), z: 8, core: 2. Of those that a mesh axis runs over, the one named last changes fastest.
Arguments:
- image: bfloat16 [4, 256, 128, 1024], P('rep', 'rows', 'cols'), may hold values from -6 to 6
- cotangent: bfloat16 [4, 256, 128, 1024], P('rep', 'rows', 'cols'), may hold values from -6 to 6
- gain: float32 [1024], replicated, may hold values from 0.5 to 1.5
- w_qkv: bfloat16 [1024, 1536], replicated, may hold values from -0.1875 to 0.1875
- w_out: bfloat16 [512, 1024], replicated, may hold values from -0.25 to 0.25
- bias_table: float32 [8, 15, 15], replicated, may hold values from -4 to 300
Outputs:
- output: bfloat16 [4, 256, 128, 1024], P('rep', 'rows', 'cols')
- grad_image: bfloat16 [4, 256, 128, 1024], P('rep', 'rows', 'cols')
- grad_qkv: float32 [1024, 1536], P(('rows', 'cols', 'rep'))
- grad_out: float32 [512, 1024], P(None, ('rows', 'cols', 'rep'))
- grad_gain: float32 [1024], P(('rows', 'cols', 'rep'))
All inputs are finite; a program needn't handle non-finite values.
Results may differ from a plain program's by a relative error of at most 0.0091.
Values may be sent and summed in bfloat16 or wider, within the bound.
A program may use at most 128 MiB of HBM per device.

v0:
```python
import jax
import jax.numpy as jnp
import numpy as np
from jax import lax
from jax.sharding import PartitionSpec as P

SHIFT = 4


EPS = 1e-06


def passed_along(value, axis, steps):
    count = lax.axis_size(axis)
    pairs = [(source, (source + steps) % count) for source in range(count)]
    return lax.ppermute(value, axis, pairs)


def offset_tables(window):
    position = np.arange(window * window)
    row_pos = position // window
    col_pos = position % window
    row_offset = row_pos[:, None] - row_pos[None, :] + window - 1
    col_offset = col_pos[:, None] - col_pos[None, :] + window - 1
    return (row_offset, col_offset)


def to_windows(tokens, window):
    rows_n, cols_n, chans = tokens.shape
    blocks = tokens.reshape(rows_n // window, window, cols_n // window, window, chans)
    return blocks.transpose(0, 2, 1, 3, 4).reshape(-1, window * window, chans)


def from_windows(blocks, rows_n, cols_n, window):
    chans = blocks.shape[-1]
    grid = blocks.reshape(rows_n // window, cols_n // window, window, window, chans)
    return grid.transpose(0, 2, 1, 3, 4).reshape(rows_n, cols_n, chans)


def contract(left, right, left_dim, right_dim):
    return lax.dot_general(
        left, right, (((left_dim,), (right_dim,)), ((), ())), preferred_element_type=jnp.float32
    )


def window_block(shifted, grad_shifted, gain, w_qkv, w_out, bias_table):
    f32 = jnp.float32
    bf16 = jnp.bfloat16
    rows_n, cols_n, features = shifted.shape
    head_count = bias_table.shape[0]
    window = (bias_table.shape[1] + 1) // 2
    all_heads = w_out.shape[0]
    head_size = all_heads // head_count
    score_scale = head_size ** (-0.5)
    flat_rows = shifted.reshape(rows_n * cols_n, features).astype(f32)
    inverse = lax.rsqrt(jnp.mean(flat_rows * flat_rows, axis=1, keepdims=True) + EPS)
    unit_rows = flat_rows * inverse
    normed = (unit_rows * gain).astype(bf16)
    projected = jnp.dot(normed, w_qkv, preferred_element_type=f32).astype(bf16)
    win_proj = to_windows(projected.reshape(rows_n, cols_n, 3 * all_heads), window)
    count_win = win_proj.shape[0]
    win_proj = win_proj.reshape(count_win, window * window, 3, head_count, head_size)
    queries = win_proj[:, :, 0]
    keys_win = win_proj[:, :, 1]
    values_win = win_proj[:, :, 2]
    row_offset, col_offset = offset_tables(window)
    bias = bias_table[:, row_offset, col_offset]
    scores = (
        jnp.einsum("nqhe,nkhe->nhqk", queries, keys_win, preferred_element_type=f32) * score_scale
        + bias[None]
    )
    peak = jnp.max(scores, axis=-1, keepdims=True)
    expo = jnp.exp(scores - peak)
    softmax_f = expo / jnp.sum(expo, axis=-1, keepdims=True)
    softmax_b = softmax_f.astype(bf16)
    heads_win = jnp.einsum(
        "nhqk,nkhe->nqhe", softmax_b, values_win, preferred_element_type=f32
    ).astype(bf16)
    heads_out = from_windows(
        heads_win.reshape(count_win, window * window, all_heads), rows_n, cols_n, window
    )
    heads_out = heads_out.reshape(rows_n * cols_n, all_heads)
    attention = jnp.dot(heads_out, w_out, preferred_element_type=f32).astype(bf16)
    upstream = grad_shifted.reshape(rows_n * cols_n, features)
    part_out_t = contract(upstream, heads_out, 0, 0)
    grad_heads = contract(upstream, w_out, 1, 1).astype(bf16)
    grad_win = to_windows(grad_heads.reshape(rows_n, cols_n, all_heads), window)
    grad_win = grad_win.reshape(count_win, window * window, head_count, head_size)
    grad_probs = jnp.einsum("nqhe,nkhe->nhqk", grad_win, values_win, preferred_element_type=f32)
    grad_values = jnp.einsum(
        "nhqk,nqhe->nkhe", softmax_b, grad_win, preferred_element_type=f32
    ).astype(bf16)
    inner = jnp.sum(grad_probs * softmax_f, axis=-1, keepdims=True)
    grad_scores = (softmax_f * (grad_probs - inner) * score_scale).astype(bf16)
    grad_queries = jnp.einsum(
        "nhqk,nkhe->nqhe", grad_scores, keys_win, preferred_element_type=f32
    ).astype(bf16)
    grad_keys = jnp.einsum(
        "nhqk,nqhe->nkhe", grad_scores, queries, preferred_element_type=f32
    ).astype(bf16)
    grad_projected = jnp.stack([grad_queries, grad_keys, grad_values], axis=2)
    grad_projected = grad_projected.reshape(count_win, window * window, 3 * all_heads)
    grad_projected = from_windows(grad_projected, rows_n, cols_n, window).reshape(
        rows_n * cols_n, 3 * all_heads
    )
    part_qkv = contract(normed, grad_projected, 0, 0)
    grad_normed = contract(grad_projected, w_qkv, 1, 1)
    part_gain = jnp.sum(grad_normed * unit_rows, axis=0)
    grad_unit = grad_normed * gain
    grad_tokens = inverse * (
        grad_unit - unit_rows * jnp.mean(grad_unit * unit_rows, axis=1, keepdims=True)
    )
    grad_tokens = grad_tokens.astype(bf16)
    return (
        attention.reshape(rows_n, cols_n, features),
        grad_tokens.reshape(rows_n, cols_n, features),
        part_qkv,
        part_out_t,
        part_gain,
    )


def pull_rows(paired):
    rim_rows = passed_along(paired[:, :SHIFT], "rows", -1)
    return jnp.concatenate([paired[:, SHIFT:], rim_rows], axis=1)


def pull_cols(paired):
    rim_cols = passed_along(paired[:, :, :SHIFT], "cols", -1)
    return jnp.concatenate([paired[:, :, SHIFT:], rim_cols], axis=2)


def push_rows(paired):
    rim_rows = passed_along(paired[:, -SHIFT:], "rows", 1)
    return jnp.concatenate([rim_rows, paired[:, :-SHIFT]], axis=1)


def push_cols(paired):
    rim_cols = passed_along(paired[:, :, -SHIFT:], "cols", 1)
    return jnp.concatenate([rim_cols, paired[:, :, :-SHIFT]], axis=2)


def local(image, cotangent, gain, w_qkv, w_out, bias_table):
    f32 = jnp.float32
    paired = jnp.stack([image[0], cotangent[0]])
    shifted = pull_cols(pull_rows(paired))
    attention, grad_tokens, part_qkv, part_out_t, part_gain = window_block(
        shifted[0], shifted[1], gain, w_qkv, w_out, bias_table
    )
    branch = jnp.stack([attention, grad_tokens])
    returned = push_cols(push_rows(branch))
    result = (image[0].astype(f32) + returned[0].astype(f32)).astype(jnp.bfloat16)
    grad_result = (cotangent[0].astype(f32) + returned[1].astype(f32)).astype(jnp.bfloat16)
    summed_qkv, summed_out, summed_gain = (
        lax.psum_scatter(part_qkv, ("rows", "cols", "rep"), scatter_dimension=0, tiled=True),
        lax.psum_scatter(part_out_t, ("rows", "cols", "rep"), scatter_dimension=0, tiled=True),
        lax.psum_scatter(part_gain, ("rows", "cols", "rep"), scatter_dimension=0, tiled=True),
    )
    total_count = (
        lax.axis_size("rows")
        * lax.axis_size("cols")
        * lax.axis_size("rep")
        * image.shape[1]
        * image.shape[2]
    )
    factor = 1.0 / float(np.sqrt(total_count))
    return (
        result[None],
        grad_result[None],
        summed_qkv * factor,
        (summed_out * factor).T,
        summed_gain * factor,
    )


def solution(mesh):
    in_specs = (P("rep", "rows", "cols", None), P("rep", "rows", "cols", None), P(), P(), P(), P())
    out_specs = (
        P("rep", "rows", "cols", None),
        P("rep", "rows", "cols", None),
        P(("rows", "cols", "rep"), None),
        P(None, ("rows", "cols", "rep")),
        P(("rows", "cols", "rep")),
    )
    return jax.shard_map(local, mesh=mesh, in_specs=in_specs, out_specs=out_specs, check_vma=False)
```

profile of v0, /device:TPU:1, one launch (start us, length us, event | category | flops | bytes accessed | tf_op | source)
XLA Modules:
  0.0 451.5 jit_solution(1420206008160629373)
XLA Ops:
  9.1 9.1 %collective-permute-start = (bf16[2,4,32,1024]{3,2,1,0:T(8,128)(2,1)S(1)}, bf16[2,4,32,1024]{3,2,1,0:T(8,128)(2,1)S(1)}, u32[]{:S(2)}, u32[]{:S(2)}) collective-permute-start(bf16[2,4,32,1024]{3,2,1,0:T(8,128)(2,1)S(1)} %slice.63), channel_id=1, source_target_pairs={{0,240},{16,0},{32,16},{48,32},{64,48},{80,64},{96,80},{112,96},{1... | collective-permute-start | bytes 1572872 | tf_op jit(solution)/shard_map/ppermute | solution.py:16
  18.4 10.4 %collective-permute-done = bf16[2,4,32,1024]{3,2,1,0:T(8,128)(2,1)S(1)} collective-permute-done((bf16[2,4,32,1024]{3,2,1,0:T(8,128)(2,1)S(1)}, bf16[2,4,32,1024]{3,2,1,0:T(8,128)(2,1)S(1)}, u32[]{:S(2)}, u32[]{:S(2)}) %collective-permute-start) | collective-permute-done | bytes 524320 | tf_op jit(solution)/shard_map/ppermute | solution.py:16
  32.2 44.6 %gather_fusion = f32[4096,8]{1,0:T(8,128)} fusion(f32[8,15,15]{0,2,1:T(8,128)S(1)} %copy.50, s32[4096]{0:T(1024)S(1)} %copy-done.1), kind=kCustom, calls=%fused_computation | custom fusion | bytes 294912 | tf_op jit(solution)/shard_map/gather | solution.py:67
  76.8 3.4 copy.51
  80.2 2.1 slice_maximum_fusion
  88.2 2.4 reshape_reshape.29
  90.6 2.5 copy.62
  93.1 2.6 multiply_convert_fusion
  96.0 1.8 convolution_convert_fusion
  99.1 5.1 %reshape_reshape.25 = bf16[8,64,3,8,64]{4,3,2,1,0:T(8,128)(2,1)} reshape(bf16[2,4,8,8,1536]{4,3,2,1,0:T(8,128)(2,1)} %bitcast.101) | data formatting | bytes 3145728 | tf_op jit(solution)/shard_map/reshape;reshape | solution.py:62
  104.1 3.6 fusion.45
  107.8 2.4 copy.73
  110.2 3.4 fusion.28
  113.6 4.0 fusion.46
  117.6 3.7 fusion.20
  122.8 5.7 %fusion.24 = bf16[8,64,1,8,64]{1,4,3,0,2:T(8,128)(2,1)} fusion(f32[8,8,64,64]{2,3,1,0:T(8,128)} %fusion.28, bf16[8,64,1,8,64]{4,3,2,1,0:T(8,128)(2,1)} %get-tuple-element.12, f32[8,8,64,64]{2,3,1,0:T(8,128)} %get-tuple-element.17, f32[8,8,64]{2,1,0:T(8,128)S(1)} %get-tuple-element.16), kind=kOutput, calls=%fused_computation.37 | convolution fusion | flops 35655744 | bytes 3162112 | tf_op jit(solution)/shard_map/nhqk,nkhe->nqhe/dot_general | solution.py:95
  128.5 5.8 %fusion.21 = bf16[8,64,1,8,64]{1,4,3,0,2:T(8,128)(2,1)} fusion(f32[8,8,64,64]{2,3,1,0:T(8,128)} %fusion.28, bf16[8,64,1,8,64]{4,3,2,1,0:T(8,128)(2,1)} %get-tuple-element.13, f32[8,8,64,64]{2,3,1,0:T(8,128)} %get-tuple-element.17, f32[8,8,64]{2,1,0:T(8,128)S(1)} %get-tuple-element.16), kind=kOutput, calls=%fused_computation.36 | convolution fusion | flops 35655744 | bytes 3162112 | tf_op jit(solution)/shard_map/nhqk,nqhe->nkhe/dot_general | solution.py:98
  134.2 2.4 copy.53
  136.7 2.6 reshape_reshape.26
  139.3 1.9 copy.54
  141.2 4.2 pad_maximum_fusion
  145.4 4.9 %copy.64 = bf16[8,64,3,8,64]{4,3,2,1,0:T(8,128)(2,1)} copy(bf16[8,64,3,8,64]{1,4,3,0,2:T(8,128)(2,1)} %pad_maximum_fusion) | data formatting | bytes 3145728 | tf_op jit(solution)/shard_map/stack | solution.py:101
  150.3 5.3 %reshape_reshape.30 = bf16[2,4,8,8,1536]{4,3,2,1,0:T(8,128)(2,1)} reshape(bf16[8,64,3,8,64]{4,3,2,1,0:T(8,128)(2,1)} %copy.64) | data formatting | bytes 3145728 | tf_op jit(solution)/shard_map/reshape;reshape | solution.py:36
  155.6 1.7 copy.65
  157.4 2.1 fusion.48
  159.5 4.5 fusion.47
  164.0 3.8 multiply_reduce_fusion
  169.8 22.0 %collective-permute-done.2 = bf16[2,4,32,1024]{3,2,1,0:T(8,128)(2,1)S(1)} collective-permute-done((bf16[2,4,32,1024]{3,2,1,0:T(8,128)(2,1)S(1)}, bf16[2,4,32,1024]{3,2,1,0:T(8,128)(2,1)S(1)}, u32[]{:S(2)}, u32[]{:S(2)}) %collective-permute-start.2) | collective-permute-done | bytes 524320 | tf_op jit(solution)/shard_map/ppermute | solution.py:16
  193.7 75.5 %all-reduce.2 = f32[1024]{0:T(1024)S(1)} all-reduce(f32[1024]{0:T(1024)S(1)} %get-tuple-element.5), channel_id=4, replica_groups=mesh['rows'=16,'cols'=4,'rep'=4] {'rows','cols','rep'}, use_global_device_ids=true, to_apply=%region_8.0.clone | all-reduce | flops 1024 | bytes 8192
  269.8 2.7 fusion.2
  272.5 2.3 add_convert_fusion
  274.8 167.1 %all-reduce.6.cloned.1.call-done = (f32[1024,1536]{1,0:T(8,128)}, f32[1024,512]{1,0:T(8,128)}) async-done(((f32[1024,1536]{1,0:T(8,128)}, f32[1024,512]{1,0:T(8,128)}), (f32[1024,1536]{1,0:T(8,128)}, f32[1024,512]{1,0:T(8,128)})) %all-reduce.6.cloned.1.call-update) | async-done | bytes 8388624
  (80 shorter events, 21.6 us)
Async XLA Ops:
  7.2 88.8 %copy-start = (bf16[1024,1536]{1,0:T(8,128)(2,1)S(1)}, bf16[1024,1536]{1,0:T(8,128)(2,1)}, u32[]{:S(2)}) copy-start(bf16[1024,1536]{1,0:T(8,128)(2,1)} %param.13) | copy-start | bytes 9437188
  7.2 434.8 %all-reduce.6.cloned.1.call-start = ((), (), s32[]{:S(2)}) async-start(), calls=%async_computation | async-start | bytes 16777216
  7.2 1.7 copy-start.10
  9.1 23.1 %copy-start.1 = (s32[4096]{0:T(1024)S(1)}, s32[4096]{0:T(1024)}, u32[]{:S(2)}) copy-start(s32[4096]{0:T(1024)} %constant.52) | copy-start | bytes 49156
  9.1 19.7 %collective-permute-start = (bf16[2,4,32,1024]{3,2,1,0:T(8,128)(2,1)S(1)}, bf16[2,4,32,1024]{3,2,1,0:T(8,128)(2,1)S(1)}, u32[]{:S(2)}, u32[]{:S(2)}) collective-permute-start(bf16[2,4,32,1024]{3,2,1,0:T(8,128)(2,1)S(1)} %slice.63), channel_id=1, source_target_pairs={{0,240},{16,0},{32,16},{48,32},{64,48},{80,64},{96,80},{112,96},{1... | collective-permute-start | bytes 1572872 | tf_op jit(solution)/shard_map/ppermute | solution.py:16
  18.4 11.3 %copy-start.6 = (bf16[2,12,32,1024]{3,2,1,0:T(8,128)(2,1)}, bf16[2,12,32,1024]{3,2,1,0:T(8,128)(2,1)S(1)}, u32[]{:S(2)}) copy-start(bf16[2,12,32,1024]{3,2,1,0:T(8,128)(2,1)S(1)} %slice.62) | copy-start | bytes 4718596
  28.8 0.9 copy-start.17
  29.7 52.7 %collective-permute-start.1 = (bf16[2,16,4,1024]{3,2,1,0:T(4,128)(2,1)}, bf16[2,16,4,1024]{3,2,1,0:T(4,128)(2,1)S(1)}, u32[]{:S(2)}, u32[]{:S(2)}) collective-permute-start(bf16[2,16,4,1024]{3,2,1,0:T(4,128)(2,1)} %pad_maximum_fusion.6), channel_id=1, source_target_pairs={{0,12},{4,0},{8,4},{12,8},{1,13},{5,1},{9,5},{13,9},{2,14},{6,2},{... | collective-permute-start | bytes 786440 | tf_op jit(solution)/shard_map/ppermute | solution.py:16
  82.4 1.3 copy-start.2
  85.1 1.5 copy-start.22
  86.6 1.6 copy-start.8
  88.2 4.8 %copy-start.21 = (f32[1024]{0:T(1024)S(1)}, f32[1024]{0:T(1024)}, u32[]{:S(2)}) copy-start(f32[1024]{0:T(1024)} %param.12) | copy-start | bytes 12292
  93.0 2.6 copy-start.3
  110.2 3.4 copy-start.20
  117.6 3.7 copy-start.13
  117.6 3.7 copy-start.24
  155.6 1.7 copy-start.9
  155.6 1.8 copy-start.14
  157.3 2.2 copy-start.18
  157.3 2.2 copy-start.19
  164.0 3.9 copy-start.15
  164.0 3.9 copy-start.23
  167.8 1.2 copy-start.4
  168.6 23.2 %copy-start.7 = (bf16[512,1024]{1,0:T(8,128)(2,1)}, bf16[512,1024]{1,0:T(8,128)(2,1)S(1)}, u32[]{:S(2)}) copy-start(bf16[512,1024]{1,0:T(8,128)(2,1)S(1)} %convolution_convert_fusion.3) | copy-start | bytes 3145732
  169.6 23.1 %copy-start.5 = (bf16[512,1024]{1,0:T(8,128)(2,1)}, bf16[512,1024]{1,0:T(8,128)(2,1)S(1)}, u32[]{:S(2)}) copy-start(bf16[512,1024]{1,0:T(8,128)(2,1)S(1)} %multiply_convert_fusion.1) | copy-start | bytes 3145732
  169.7 22.1 %collective-permute-start.2 = (bf16[2,4,32,1024]{3,2,1,0:T(8,128)(2,1)S(1)}, bf16[2,4,32,1024]{3,2,1,0:T(8,128)(2,1)S(1)}, u32[]{:S(2)}, u32[]{:S(2)}) collective-permute-start(bf16[2,4,32,1024]{3,2,1,0:T(8,128)(2,1)S(1)} %pad_maximum_fusion.4), channel_id=1, source_target_pairs={{0,16},{16,32},{32,48},{48,64},{64,80},{80,96},{96,112},{112,128},... | collective-permute-start | bytes 1572872 | tf_op jit(solution)/shard_map/ppermute | solution.py:16
  191.8 2.0 copy-start.16
  192.7 77.1 %collective-permute-start.3 = (bf16[2,16,4,1024]{3,2,1,0:T(4,128)(2,1)}, bf16[2,16,4,1024]{3,2,1,0:T(4,128)(2,1)S(1)}, u32[]{:S(2)}, u32[]{:S(2)}) collective-permute-start(bf16[2,16,4,1024]{3,2,1,0:T(4,128)(2,1)} %pad_maximum_fusion.5), channel_id=1, source_target_pairs={{0,4},{4,8},{8,12},{12,0},{1,5},{5,9},{9,13},{13,1},{2,6},{6,10},{... | collective-permute-start | bytes 786440 | tf_op jit(solution)/shard_map/ppermute | solution.py:16
  269.8 2.7 copy-start.11
  269.8 2.7 copy-start.12
Sparse Core Ops, SparseCore 0:
  164.1 277.7 all-reduce.5
where the time goes:
time: 453 us; the launch traced here: 452 us
  waiting for transfers between devices  200 us (44%)
  local copies, waits for them, and re-layouts  90 us (20%)
  blocking collectives  75.5 us (17%)
  matrix products  37.6 us (8%)
  other arithmetic  22.7 us (5%)
  between operations  14.3 us (3%)
  starting transfers between devices  11.8 us (3%)
    unnamed x2, waiting for transfers between devices  167 us
    unnamed x1, blocking collectives  75.5 us
    gather x2, local copies, waits for them, and re-layouts, window_block(): bias = bias_table[:, row_offset, col_offset]  48 us
    ppermute x4, waiting for transfers between devices, passed_along(): return lax.ppermute(value, axis, pairs)  32.4 us
    ppermute x4, starting transfers between devices, passed_along(): return lax.ppermute(value, axis, pairs)  11.8 us
    dot_general x4, matrix products, contract(): lax.dot_general(left, right, (((left_dim,), (right_dim,)), ((), ())), pre...  11.1 us
  transfers between devices with their start and end apart: 5, of which 3 were waited for; matrix products, arithmetic and copies ran while one was open for 14% of the time, Pallas kernels for 0%

commit v1 on v0

--- a/solution.py
+++ b/solution.py
@@ -1,8 +1,14 @@
+import functools
+
 import jax
 import jax.numpy as jnp
 import numpy as np
 from jax import lax
+from jax.experimental import pallas as pl
+from jax.experimental.pallas import tpu as pltpu
 from jax.sharding import PartitionSpec as P
+
+MESH = pl.DeviceIdType.MESH
 
 SHIFT = 4
 
@@ -140,6 +146,189 @@
     return jnp.concatenate([rim_cols, paired[:, :, :-SHIFT]], axis=2)
 
 
+def rs_kernel(nz, nx, m_ref, out_ref, recv0, acc_x, acc_y, acc_z,
+              rx1, ax1, rx2, ax2, rx3, ry1, ay1, ry2, ay2, ry3, rz1, az1, rz2, az2, rz3,
+              swap_out, swap_in, sends, recvs):
+    f32, bf16 = jnp.float32, jnp.bfloat16
+    row, col, x = lax.axis_index("rows"), lax.axis_index("cols"), lax.axis_index("rep")
+    yh, z = row // nz, row % nz
+    yl, core = col // 2, col % 2
+    y = yh * 2 + yl
+    slot = iter(range(1000))
+    pair = (row, yl * 2 + 1 - core, x)
+
+    def on_x(step):
+        other = (x + step) % nx
+        return other, (row, col, other)
+
+    def on_y(step):
+        other = (y + step) % 4
+        return (other // 2, other % 2), ((other // 2) * nz + z, (other % 2) * 2 + core, x)
+
+    def on_z(step):
+        other = (z + step) % nz
+        return other, (yh * nz + other, col, x)
+
+    barrier = pltpu.get_barrier_semaphore()
+    peers = [pair]
+    peers += [on_x(step)[1] for step in range(1, nx)]
+    peers += [on_y(step)[1] for step in range(1, 4)]
+    peers += [on_z(step)[1] for step in range(1, nz)]
+    for peer in peers:
+        pl.semaphore_signal(barrier, inc=1, device_id=peer, device_id_type=MESH)
+    pl.semaphore_wait(barrier, len(peers))
+
+    started = []
+
+    def send(source, target, device):
+        index = next(slot)
+        copy = pltpu.make_async_remote_copy(
+            src_ref=source, dst_ref=target, send_sem=sends.at[index], recv_sem=recvs.at[index],
+            device_id=device, device_id_type=MESH)
+        copy.start()
+        started.append(copy)
+        return copy
+
+    cols_z, cols_x, cols_y = pl.ds(1536, 512), pl.ds(0, 1024), pl.ds(1024, 512)
+    first = {}
+    for name, cols in (("z", cols_z), ("x", cols_x), ("y", cols_y)):
+        first[name] = send(m_ref.at[:, :, :, 1 - core, :, cols], recv0.at[:, :, :, :, cols], pair)
+
+    def add_pair(name):
+        first[name].wait_recv()
+
+        def body(block, carry):
+            a, b, c = block // (2 * nz), (block // 2) % nz, block % 2
+            if name == "z":
+                acc_z[a, b, c] = m_ref[a, b, c, core, :, 1536:2048] + recv0[a, b, c, :, 1536:2048]
+            elif name == "y":
+                acc_y[a, b, c] = m_ref[a, b, c, core, :, 1024:1536] + recv0[a, b, c, :, 1024:1536]
+            else:
+                wide = 1024 // nx
+                for part in range(nx):
+                    lo = part * wide
+                    acc_x[part, a, b, c] = m_ref[a, b, c, core, :, lo:lo + wide] + recv0[a, b, c, :, lo:lo + wide]
+            return carry
+
+        lax.fori_loop(0, 4 * nz, body, 0)
+
+    def landed(copies):
+        for copy in copies:
+            copy.wait_recv()
+
+    def total(own, slots, count):
+        value = own.astype(f32)
+        for k in range(count):
+            value = value + slots[k].astype(f32)
+        return value
+
+    add_pair("z")
+    z1 = [send(acc_z.at[:, on_z(s)[0]], rz1.at[s - 1], on_z(s)[1]) for s in range(1, nz)]
+    add_pair("x")
+    x1 = [send(acc_x.at[on_x(s)[0]], rx1.at[s - 1], on_x(s)[1]) for s in range(1, nx)]
+    add_pair("y")
+    y1 = [send(acc_y.at[on_y(s)[0][0], :, on_y(s)[0][1]], ry1.at[s - 1], on_y(s)[1]) for s in range(1, 4)]
+
+    landed(y1)
+
+    def body_y1(b, carry):
+        ay1[b] = total(acc_y[yh, b, yl], [ry1[k, b] for k in range(3)], 3).astype(bf16)
+        return carry
+
+    lax.fori_loop(0, nz, body_y1, 0)
+    y2 = [send(ay1.at[on_z(s)[0]], ry2.at[s - 1], on_z(s)[1]) for s in range(1, nz)]
+
+    landed(x1)
+
+    def body_x1(block, carry):
+        a, b, c = block // (2 * nz), (block // 2) % nz, block % 2
+        ax1[a, b, c] = total(acc_x[x, a, b, c], [rx1[k, a, b, c] for k in range(nx - 1)], nx - 1).astype(bf16)
+        return carry
+
+    lax.fori_loop(0, 4 * nz, body_x1, 0)
+    x2 = [send(ax1.at[on_y(s)[0][0], :, on_y(s)[0][1]], rx2.at[s - 1], on_y(s)[1]) for s in range(1, 4)]
+
+    landed(z1)
+    for a in range(2):
+        for c in range(2):
+            value = total(acc_z[a, z, c], [rz1[k, a, c] for k in range(nz - 1)], nz - 1).astype(bf16)
+            wide = 512 // nx
+            for part in range(nx):
+                az1[part, a, c] = value[:, part * wide:(part + 1) * wide]
+    z2 = [send(az1.at[on_x(s)[0]], rz2.at[s - 1], on_x(s)[1]) for s in range(1, nx)]
+
+    landed(y2)
+    value = total(ay1[z], [ry2[k] for k in range(nz - 1)], nz - 1).astype(bf16)
+    wide = 512 // nx
+    for part in range(nx):
+        ay2[part] = value[:, part * wide:(part + 1) * wide]
+    y3 = [send(ay2.at[on_x(s)[0]], ry3.at[s - 1], on_x(s)[1]) for s in range(1, nx)]
+    landed(x2)
+
+    def body_x2(b, carry):
+        ax2[b] = total(ax1[yh, b, yl], [rx2[k, b] for k in range(3)], 3).astype(bf16)
+        return carry
+
+    lax.fori_loop(0, nz, body_x2, 0)
+    x3 = [send(ax2.at[on_z(s)[0]], rx3.at[s - 1], on_z(s)[1]) for s in range(1, nz)]
+    landed(z2)
+    for a in range(2):
+        for c in range(2):
+            az2[a, c] = total(az1[x, a, c], [rz2[k, a, c] for k in range(nx - 1)], nx - 1).astype(bf16)
+    z3 = [send(az2.at[on_y(s)[0][0], on_y(s)[0][1]], rz3.at[s - 1], on_y(s)[1]) for s in range(1, 4)]
+
+    landed(y3)
+    sum_y = total(ay2[x], [ry3[k] for k in range(nx - 1)], nx - 1)
+    landed(z3)
+    sum_z = total(az2[yh, yl], [rz3[k] for k in range(3)], 3)
+    landed(x3)
+    sum_x = total(ax2[z], [rx3[k] for k in range(nz - 1)], nz - 1)
+    rest = jnp.concatenate([sum_y, sum_z], axis=1)
+    for other in range(nx):
+        swap_out[other, 0:4] = sum_x[other * 4:other * 4 + 4]
+        swap_out[other, 4:8] = rest[other * 4:other * 4 + 4]
+    last = [send(swap_out.at[on_x(s)[0]], swap_in.at[s - 1], on_x(s)[1]) for s in range(1, nx)]
+    swap_in[nx - 1] = swap_out[x]
+    landed(last)
+    for source in range(nx):
+        k = (x - source + nx - 1) % nx
+        got = swap_in[k]
+        wx, wr = 1024 // nx, 512 // nx
+        out_ref[:, source * wx:(source + 1) * wx] = got[0:4]
+        out_ref[:, 1024 + source * wr:1024 + (source + 1) * wr] = got[4:8, 0:wr]
+        out_ref[:, 1536 + source * wr:1536 + (source + 1) * wr] = got[4:8, wr:2 * wr]
+    for copy in started:
+        copy.wait_send()
+
+
+def reduce_scatter(partial, nz, nx):
+    bf16, f32 = jnp.bfloat16, jnp.float32
+    wx, wr = 1024 // nx, 512 // nx
+    shapes = [
+        ((2, nz, 2, 16, 2048), bf16),
+        ((nx, 2, nz, 2, 16, wx), bf16), ((2, nz, 2, 16, 512), bf16), ((2, nz, 2, 16, 512), bf16),
+        ((nx - 1, 2, nz, 2, 16, wx), bf16), ((2, nz, 2, 16, wx), bf16),
+        ((3, nz, 16, wx), bf16), ((nz, 16, wx), bf16), ((nz - 1, 16, wx), bf16),
+        ((3, nz, 16, 512), bf16), ((nz, 16, 512), bf16),
+        ((nz - 1, 16, 512), bf16), ((nx, 16, wr), bf16), ((nx - 1, 16, wr), bf16),
+        ((nz - 1, 2, 2, 16, 512), bf16), ((nx, 2, 2, 16, wr), bf16),
+        ((nx - 1, 2, 2, 16, wr), bf16), ((2, 2, 16, wr), bf16), ((3, 16, wr), bf16),
+        ((nx, 8, wx), f32), ((nx, 8, wx), f32),
+    ]
+    copies = 3 + (nz - 1 + nx - 1 + 3) * 3 + nx - 1
+    return pl.pallas_call(
+        functools.partial(rs_kernel, nz, nx),
+        out_shape=jax.ShapeDtypeStruct((4, 2048), f32),
+        in_specs=[pl.BlockSpec(memory_space=pltpu.VMEM)],
+        out_specs=pl.BlockSpec(memory_space=pltpu.VMEM),
+        scratch_shapes=[pltpu.VMEM(shape, kind) for shape, kind in shapes]
+        + [pltpu.SemaphoreType.DMA((copies,)), pltpu.SemaphoreType.DMA((copies,))],
+        compiler_params=pltpu.CompilerParams(
+            collective_id=0, has_side_effects=True, vmem_limit_bytes=40 * 1024 * 1024),
+        name="reduce_scatter",
+    )(partial.reshape(2, nz, 2, 2, 16, 2048))
+
+
 def local(image, cotangent, gain, w_qkv, w_out, bias_table):
     f32 = jnp.float32
     paired = jnp.stack([image[0], cotangent[0]])
@@ -151,11 +340,8 @@
     returned = push_cols(push_rows(branch))
     result = (image[0].astype(f32) + returned[0].astype(f32)).astype(jnp.bfloat16)
     grad_result = (cotangent[0].astype(f32) + returned[1].astype(f32)).astype(jnp.bfloat16)
-    summed_qkv, summed_out, summed_gain = (
-        lax.psum_scatter(part_qkv, ("rows", "cols", "rep"), scatter_dimension=0, tiled=True),
-        lax.psum_scatter(part_out_t, ("rows", "cols", "rep"), scatter_dimension=0, tiled=True),
-        lax.psum_scatter(part_gain, ("rows", "cols", "rep"), scatter_dimension=0, tiled=True),
-    )
+    partial = jnp.concatenate([part_qkv.astype(jnp.bfloat16), part_out_t.astype(jnp.bfloat16)], axis=1)
+    summed = reduce_scatter(partial, lax.axis_size("rows") // 2, lax.axis_size("rep"))
     total_count = (
         lax.axis_size("rows")
         * lax.axis_size("cols")
@@ -164,12 +350,17 @@
         * image.shape[2]
     )
     factor = 1.0 / float(np.sqrt(total_count))
+    grad_qkv = summed[:, :1536] * factor
+    first = 4 * ((lax.axis_index("rows") * 4 + lax.axis_index("cols")) * 4 + lax.axis_index("rep"))
+    own_w = lax.dynamic_slice_in_dim(w_qkv, first, 4, 0).astype(f32)
+    own_gain = lax.dynamic_slice_in_dim(gain, first, 4, 0)
+    grad_gain = jnp.sum(own_w * grad_qkv, axis=1) / own_gain
     return (
         result[None],
         grad_result[None],
-        summed_qkv * factor,
-        (summed_out * factor).T,
-        summed_gain * factor,
+        grad_qkv,
+        (summed[:, 1536:] * factor).T,
+        grad_gain,
     )
 
 

time: 453 us -> 184 us (0.41)
  waiting for transfers between devices: 200 us -> 12.5 us
  blocking collectives: 75.5 us -> 0 us
  Pallas kernels: 0 us -> 37 us
  local copies, waits for them, and re-layouts: 90 us -> 65.4 us
  between operations: 14.3 us -> 0.97 us
  other arithmetic: 22.7 us -> 16.3 us
    unnamed x2 -> x0, waiting for transfers between devices: 167 us -> none
    unnamed x1 -> x0, blocking collectives: 75.5 us -> none
    pallas_call x0 -> x1, Pallas kernels: none -> 37 us  [reduce_scatter(): pl.pallas_call(functools.partial(rs_kernel, nz, nx), out_shape=jax.ShapeD...]
    gather x2, local copies, waits for them, and re-layouts: 48 us -> 27.4 us  [window_block(): bias = bias_table[:, row_offset, col_offset]]
    ppermute x4, waiting for transfers between devices: 32.4 us -> 12.5 us  [passed_along(): return lax.ppermute(value, axis, pairs)]
  transfers between devices with their start and end apart: 5 -> 4, of which waited for: 3 -> 2; matrix products, arithmetic and copies ran while one was open for 14% -> 18% of each run, Pallas kernels for 0% -> 0%
where the time goes in v1:
time: 184 us; the launch traced here: 182 us
  local copies, waits for them, and re-layouts  65.4 us (36%)
  Pallas kernels  37 us (20%)
  matrix products  35 us (19%)
  other arithmetic  16.3 us (9%)
  starting transfers between devices  14.7 us (8%)
  waiting for transfers between devices  12.5 us (7%)
    pallas_call x1, Pallas kernels, reduce_scatter(): pl.pallas_call(functools.partial(rs_kernel, nz, nx), out_shape=jax.ShapeD...  37 us
    gather x2, local copies, waits for them, and re-layouts, window_block(): bias = bias_table[:, row_offset, col_offset]  27.4 us
    ppermute x4, starting transfers between devices, passed_along(): return lax.ppermute(value, axis, pairs)  14.7 us
    ppermute x4, waiting for transfers between devices, passed_along(): return lax.ppermute(value, axis, pairs)  12.5 us
    dot_general x4, matrix products, contract(): lax.dot_general(left, right, (((left_dim,), (right_dim,)), ((), ())), pre...  7.53 us
    unnamed x51, local copies, waits for them, and re-layouts  7.47 us
    another operation x2, local copies, waits for them, and re-layouts, from_windows(): blocks.reshape(rows_n // window, cols_n // window, window, window, chans)  6.73 us
    dot_general x1, matrix products, window_block(): jnp.einsum('nhqk,nkhe->nqhe', grad_scores, keys_win, preferred_element_ty...  5.73 us
  transfers between devices with their start and end apart: 4, of which 2 were waited for; matrix products, arithmetic and copies ran while one was open for 18% of the time, Pallas kernels for 0%

profile of v1, /device:TPU:1, one launch (start us, length us, event | category | flops | bytes accessed | tf_op | source)
XLA Modules:
  0.0 181.9 jit_solution(3930955509126334428)
XLA Ops:
  0.7 1.5 constant_dynamic-update-slice_fusion.1
  2.4 9.1 %collective-permute-start = (bf16[2,4,32,1024]{3,2,1,0:T(8,128)(2,1)S(1)}, bf16[2,4,32,1024]{3,2,1,0:T(8,128)(2,1)S(1)}, u32[]{:S(2)}, u32[]{:S(2)}) collective-permute-start(bf16[2,4,32,1024]{3,2,1,0:T(8,128)(2,1)S(1)} %slice.71), channel_id=1, source_target_pairs={{0,240},{16,0},{32,16},{48,32},{64,48},{80,64},{96,80},{112,96},{1... | collective-permute-start | bytes 1572872 | tf_op jit(solution)/shard_map/ppermute | solution.py:22
  11.8 10.4 %collective-permute-done = bf16[2,4,32,1024]{3,2,1,0:T(8,128)(2,1)S(1)} collective-permute-done((bf16[2,4,32,1024]{3,2,1,0:T(8,128)(2,1)S(1)}, bf16[2,4,32,1024]{3,2,1,0:T(8,128)(2,1)S(1)}, u32[]{:S(2)}, u32[]{:S(2)}) %collective-permute-start) | collective-permute-done | bytes 524320 | tf_op jit(solution)/shard_map/ppermute | solution.py:22
  23.0 1.5 collective-permute-start.1
  24.7 25.6 %gather_fusion = f32[4096,8]{1,0:T(8,128)S(1)} fusion(f32[8,15,15]{0,2,1:T(8,128)S(1)} %copy.31, s32[4096]{0:T(1024)S(1)} %copy-done.1), kind=kCustom, calls=%fused_computation | custom fusion | bytes 294912 | tf_op jit(solution)/shard_map/gather | solution.py:73
  50.3 1.9 %copy.32 = f32[64,64,8]{0,1,2:T(8,128)} copy(f32[64,64,8]{2,1,0:T(8,128)S(1)} %bitcast.103) | data formatting | bytes 262144 | tf_op jit(solution)/shard_map/gather | solution.py:73
  52.2 2.1 %slice_maximum_fusion = bf16[2,16,28,1024]{3,2,1,0:T(8,128)(2,1)S(1)} fusion(bf16[2,4,32,1024]{3,2,1,0:T(8,128)(2,1)} %copy-done.8, bf16[2,12,32,1024]{3,2,1,0:T(8,128)(2,1)} %copy-done.3), kind=kLoop, calls=%fused_computation.10 | loop fusion | flops 917504 | bytes 3932160 | tf_op jit(solution)/shard_map/concatenate | solution.py:131
  55.7 1.5 multiply_convert_fusion.3
  57.2 3.7 %convolution_convert_fusion.1 = bf16[512,1536]{1,0:T(8,128)(2,1)S(1)} fusion(bf16[512,1024]{1,0:T(8,128)(2,1)S(1)} %multiply_convert_fusion.3, bf16[1024,1536]{1,0:T(8,128)(2,1)} %param.13), kind=kOutput, calls=%fused_computation.6 | convolution fusion | flops 1611399168 | bytes 5767168 | tf_op jit(solution)/shard_map/dot_general | solution.py:65
  62.2 5.1 %reshape_reshape.25 = bf16[8,64,3,8,64]{4,3,2,1,0:T(8,128)(2,1)} reshape(bf16[2,4,8,8,1536]{4,3,2,1,0:T(8,128)(2,1)} %bitcast.101) | data formatting | bytes 3145728 | tf_op jit(solution)/shard_map/reshape;reshape | solution.py:68
  67.3 3.6 %fusion.44 = (bf16[8,64,1,8,64]{4,3,2,1,0:T(8,128)(2,1)}, bf16[8,64,1,8,64]{4,3,2,1,0:T(8,128)(2,1)}, bf16[8,64,1,8,64]{4,3,2,1,0:T(8,128)(2,1)}) fusion(bf16[8,64,3,8,64]{4,3,2,1,0:T(8,128)(2,1)} %reshape_reshape.25), kind=kLoop, calls=%fused_computation.73 | loop fusion | bytes 3145728 | tf_op jit(solution)/shard_map/slice | solution.py:71
  70.9 2.4 %copy.56 = bf16[8,64,1,8,64]{1,4,3,0,2:T(8,128)(2,1)} copy(bf16[8,64,1,8,64]{4,3,2,1,0:T(8,128)(2,1)} %get-tuple-element.9) | data formatting | bytes 1048576
  75.1 1.7 reshape_reshape.29
  76.9 1.5 copy.43
  78.3 3.2 %fusion.28 = f32[8,8,64,64]{2,3,1,0:T(8,128)} fusion(bf16[8,64,8,64]{1,3,2,0:T(8,128)(2,1)} %copy.43, bf16[8,64,1,8,64]{1,4,3,0,2:T(8,128)(2,1)S(1)} %copy-done.7), kind=kOutput, calls=%fused_computation.45 | convolution fusion | flops 33554432 | bytes 2097152 | tf_op jit(solution)/shard_map/nqhe,nkhe->nhqk/dot_general | solution.py:95
  81.5 3.7 %fusion.45 = (f32[8,8,64]{2,1,0:T(8,128)S(1)}, f32[8,8,64,64]{2,3,1,0:T(8,128)}) fusion(f32[8,64,64]{1,2,0:T(8,128)S(1)} %bitcast.115, bf16[8,64,1,8,64]{4,3,2,1,0:T(8,128)(2,1)} %get-tuple-element.10, bf16[8,64,1,8,64]{4,3,2,1,0:T(8,128)(2,1)S(1)} %copy-done.11), kind=kOutput, calls=%fused_computation.74 | convolution fusion | flops 34603072 | bytes 2244608 | tf_op jit(solution)/shard_map/sub | solution.py:79
  85.2 5.7 %fusion.24 = bf16[8,64,1,8,64]{1,4,3,0,2:T(8,128)(2,1)} fusion(f32[8,8,64,64]{2,3,1,0:T(8,128)} %fusion.28, bf16[8,64,1,8,64]{4,3,2,1,0:T(8,128)(2,1)} %get-tuple-element.10, f32[8,8,64,64]{2,3,1,0:T(8,128)} %get-tuple-element.15, f32[8,8,64]{2,1,0:T(8,128)S(1)} %get-tuple-element.14), kind=kOutput, calls=%fused_computation.39 | convolution fusion | flops 35655744 | bytes 3162112 | tf_op jit(solution)/shard_map/nhqk,nkhe->nqhe/dot_general | solution.py:101
  90.9 5.5 %fusion.21 = bf16[8,64,1,8,64]{1,4,3,0,2:T(8,128)(2,1)} fusion(f32[8,8,64,64]{2,3,1,0:T(8,128)} %fusion.28, bf16[8,64,1,8,64]{4,3,2,1,0:T(8,128)(2,1)S(1)} %copy-done.11, f32[8,8,64,64]{2,3,1,0:T(8,128)} %get-tuple-element.15, f32[8,8,64]{2,1,0:T(8,128)S(1)} %get-tuple-element.14), kind=kOutput, calls=%fused_computation.38 | convolution fusion | flops 35655744 | bytes 3162112 | tf_op jit(solution)/shard_map/nhqk,nqhe->nkhe/dot_general | solution.py:104
  96.4 3.6 %fusion.20 = bf16[8,64,1,8,64]{1,4,3,0,2:T(8,128)(2,1)} fusion(bf16[8,64,8,64]{1,3,2,0:T(8,128)(2,1)} %copy.43, f32[8,8,64,64]{2,3,1,0:T(8,128)} %get-tuple-element.15, f32[8,8,64]{2,1,0:T(8,128)S(1)} %get-tuple-element.14), kind=kOutput, calls=%fused_computation.37 | convolution fusion | flops 34340864 | bytes 2113536 | tf_op jit(solution)/shard_map/nhqk,nqhe->nkhe/dot_general | solution.py:96
  102.0 1.4 fusion.19
  103.5 1.7 copy.34
  107.7 3.0 %convolution_convert_fusion.4 = bf16[1024,512]{1,0:T(8,128)(2,1)} fusion(bf16[512,1024]{1,0:T(8,128)(2,1)} %bitcast.110, bf16[512,512]{1,0:T(8,128)(2,1)S(1)} %bitcast.112), kind=kOutput, calls=%fused_computation.34 | convolution fusion | flops 537395200 | bytes 2621440 | tf_op jit(solution)/shard_map/dot_general | solution.py:47
  112.2 2.4 %pad_maximum_fusion.1 = bf16[8,64,3,8,64]{1,4,3,0,2:T(8,128)(2,1)} fusion(bf16[8,64,1,8,64]{1,4,3,0,2:T(8,128)(2,1)S(1)} %copy-done.14, bf16[8,64,1,8,64]{1,4,3,0,2:T(8,128)(2,1)S(1)} %copy-done.13, bf16[8,64,1,8,64]{1,4,3,0,2:T(8,128)(2,1)S(1)} %copy-done.12), kind=kLoop, calls=%fused_computation.5 | loop fusion | flops 1572864 | bytes 3145728 | tf_op jit(solution)/shard_map/stack | solution.py:107
  114.7 4.9 %copy.45 = bf16[8,64,3,8,64]{4,3,2,1,0:T(8,128)(2,1)} copy(bf16[8,64,3,8,64]{1,4,3,0,2:T(8,128)(2,1)} %pad_maximum_fusion.1) | data formatting | bytes 3145728 | tf_op jit(solution)/shard_map/stack | solution.py:107
  119.5 5.3 %reshape_reshape.30 = bf16[2,4,8,8,1536]{4,3,2,1,0:T(8,128)(2,1)} reshape(bf16[8,64,3,8,64]{4,3,2,1,0:T(8,128)(2,1)} %copy.45) | data formatting | bytes 3145728 | tf_op jit(solution)/shard_map/reshape;reshape | solution.py:42
  124.8 1.7 copy.46
  127.2 1.9 %multiply_reduce_fusion = (f32[512]{0:T(512)S(1)}, f32[512,1024]{1,0:T(8,128)S(1)}) fusion(bf16[1,16,32,1024]{3,2,1,0:T(8,128)(2,1)S(1)} %copy-done.2, f32[1024]{0:T(1024)S(1)} %copy-done.19, f32[512]{0:T(512)S(1)} %copy-done.21, bf16[512,1536]{1,0:T(8,128)(2,1)S(1)} %bitcast.106, bf16[1024,1536]{1,0:T(8,128)(2,1)S(1)} %copy-done.22), kind=kOutput, calls=%fused_computation.18 | convolution fusion | flops 1613233664 | bytes 7872512 | tf_op jit(solution)/shard_map/dot_general | solution.py:47
  129.2 1.8 %convolution_convert_fusion = bf16[1024,1536]{1,0:T(8,128)(2,1)S(1)} fusion(bf16[512,1024]{1,0:T(8,128)(2,1)S(1)} %bitcast.111, bf16[512,1536]{1,0:T(8,128)(2,1)S(1)} %bitcast.107), kind=kOutput, calls=%fused_computation.4 | convolution fusion | flops 1612185600 | bytes 5767168 | tf_op jit(solution)/shard_map/dot_general | solution.py:47
  133.4 37.0 %reduce_scatter.1 = f32[4,2048]{1,0:T(4,128)S(1)} custom-call(bf16[2,8,2,2,16,2048]{5,4,3,2,1,0:T(8,128)(2,1)S(1)} %bitcast.94), custom_call_target="tpu_custom_call" | custom-call | tf_op jit(solution)/shard_map/reduce_scatter/pallas_call | solution.py:319
  171.3 4.0 %collective-permute-start.3 = (bf16[2,16,4,1024]{3,2,1,0:T(4,128)(2,1)S(1)}, bf16[2,16,4,1024]{3,2,1,0:T(4,128)(2,1)S(1)}, u32[]{:S(2)}, u32[]{:S(2)}) collective-permute-start(bf16[2,16,4,1024]{3,2,1,0:T(4,128)(2,1)S(1)} %pad_maximum_fusion.6), channel_id=1, source_target_pairs={{0,4},{4,8},{8,12},{12,0},{1,5},{5,9},{9,13},{13,1},{2,6},{6,10},{... | collective-permute-start | bytes 786440 | tf_op jit(solution)/shard_map/ppermute | solution.py:22
  176.4 2.1 %collective-permute-done.3 = bf16[2,16,4,1024]{3,2,1,0:T(4,128)(2,1)S(1)} collective-permute-done((bf16[2,16,4,1024]{3,2,1,0:T(4,128)(2,1)S(1)}, bf16[2,16,4,1024]{3,2,1,0:T(4,128)(2,1)S(1)}, u32[]{:S(2)}, u32[]{:S(2)}) %collective-permute-start.3) | collective-permute-done | bytes 262176 | tf_op jit(solution)/shard_map/ppermute | solution.py:22
  179.6 2.3 %add_convert_fusion = (bf16[1,16,32,1024]{3,2,1,0:T(8,128)(2,1)}, bf16[1,16,32,1024]{3,2,1,0:T(8,128)(2,1)}) fusion(bf16[1,16,32,1024]{3,2,1,0:T(8,128)(2,1)S(1)} %copy-done.5, bf16[2,16,32,1024]{3,2,1,0:T(8,128)(2,1)S(1)} %fusion.2, bf16[1,16,32,1024]{3,2,1,0:T(8,128)(2,1)S(1)} %copy-done.6), kind=kLoop, calls=%fused_computation.15 | loop fusion | flops 4194304 | bytes 6291456 | tf_op jit(solution)/shard_map/convert_element_type | solution.py:342
  (76 shorter events, 18.0 us)
Async XLA Ops:
  0.6 72.9 %copy-start = (bf16[512,1024]{1,0:T(8,128)(2,1)S(1)}, bf16[512,1024]{1,0:T(8,128)(2,1)}, u32[]{:S(2)}) copy-start(bf16[512,1024]{1,0:T(8,128)(2,1)} %param.14) | copy-start | bytes 3145732
  0.6 1.6 copy-start.4
  2.4 22.2 %copy-start.17 = (f32[8,15,15]{2,0,1:T(8,128)S(1)}, f32[8,15,15]{2,0,1:T(8,128)}, u32[]{:S(2)}) copy-start(f32[8,15,15]{2,0,1:T(8,128)} %param.15) | copy-start | bytes 21604
  2.4 22.3 %copy-start.1 = (s32[4096]{0:T(1024)S(1)}, s32[4096]{0:T(1024)}, u32[]{:S(2)}) copy-start(s32[4096]{0:T(1024)} %constant.69) | copy-start | bytes 49156
  2.4 19.7 %collective-permute-start = (bf16[2,4,32,1024]{3,2,1,0:T(8,128)(2,1)S(1)}, bf16[2,4,32,1024]{3,2,1,0:T(8,128)(2,1)S(1)}, u32[]{:S(2)}, u32[]{:S(2)}) collective-permute-start(bf16[2,4,32,1024]{3,2,1,0:T(8,128)(2,1)S(1)} %slice.71), channel_id=1, source_target_pairs={{0,240},{16,0},{32,16},{48,32},{64,48},{80,64},{96,80},{112,96},{1... | collective-permute-start | bytes 1572872 | tf_op jit(solution)/shard_map/ppermute | solution.py:22
  11.7 12.8 %copy-start.3 = (bf16[2,12,32,1024]{3,2,1,0:T(8,128)(2,1)}, bf16[2,12,32,1024]{3,2,1,0:T(8,128)(2,1)S(1)}, u32[]{:S(2)}) copy-start(bf16[2,12,32,1024]{3,2,1,0:T(8,128)(2,1)S(1)} %slice.70) | copy-start | bytes 4718596
  22.1 2.4 %copy-start.8 = (bf16[2,4,32,1024]{3,2,1,0:T(8,128)(2,1)}, bf16[2,4,32,1024]{3,2,1,0:T(8,128)(2,1)S(1)}, u32[]{:S(2)}) copy-start(bf16[2,4,32,1024]{3,2,1,0:T(8,128)(2,1)S(1)} %collective-permute-done) | copy-start | bytes 1572868
  23.0 31.3 %collective-permute-start.1 = (bf16[2,16,4,1024]{3,2,1,0:T(4,128)(2,1)}, bf16[2,16,4,1024]{3,2,1,0:T(4,128)(2,1)S(1)}, u32[]{:S(2)}, u32[]{:S(2)}) collective-permute-start(bf16[2,16,4,1024]{3,2,1,0:T(4,128)(2,1)} %pad_maximum_fusion.7), channel_id=1, source_target_pairs={{0,12},{4,0},{8,4},{12,8},{1,13},{5,1},{9,5},{13,9},{2,14},{6,2},{... | collective-permute-start | bytes 786440 | tf_op jit(solution)/shard_map/ppermute | solution.py:22
  54.3 1.4 copy-start.18
  55.7 5.2 %copy-start.20 = (f32[512]{0:T(512)}, f32[512]{0:T(512)S(1)}, u32[]{:S(2)}) copy-start(f32[512]{0:T(512)S(1)} %rsqrt.13) | copy-start | bytes 6148
  73.5 1.6 copy-start.9
  75.1 3.2 %copy-start.7 = (bf16[8,64,1,8,64]{1,4,3,0,2:T(8,128)(2,1)S(1)}, bf16[8,64,1,8,64]{1,4,3,0,2:T(8,128)(2,1)}, u32[]{:S(2)}) copy-start(bf16[8,64,1,8,64]{1,4,3,0,2:T(8,128)(2,1)} %copy.56) | copy-start | bytes 1572868
  78.3 3.2 %copy-start.11 = (bf16[8,64,1,8,64]{4,3,2,1,0:T(8,128)(2,1)S(1)}, bf16[8,64,1,8,64]{4,3,2,1,0:T(8,128)(2,1)}, u32[]{:S(2)}) copy-start(bf16[8,64,1,8,64]{4,3,2,1,0:T(8,128)(2,1)} %get-tuple-element.11) | copy-start | bytes 1572868
  78.3 3.2 %copy-start.16 = (f32[64,64,8]{0,1,2:T(8,128)S(1)}, f32[64,64,8]{0,1,2:T(8,128)}, u32[]{:S(2)}) copy-start(f32[64,64,8]{0,1,2:T(8,128)} %copy.32) | copy-start | bytes 393220
  96.4 3.7 %copy-start.2 = (bf16[1,16,32,1024]{3,2,1,0:T(8,128)(2,1)S(1)}, bf16[1,16,32,1024]{3,2,1,0:T(8,128)(2,1)}, u32[]{:S(2)}) copy-start(bf16[1,16,32,1024]{3,2,1,0:T(8,128)(2,1)} %get-tuple-element.8) | copy-start | bytes 3145732
  96.4 3.7 %copy-start.19 = (f32[1024]{0:T(1024)S(1)}, f32[1024]{0:T(1024)}, u32[]{:S(2)}) copy-start(f32[1024]{0:T(1024)} %param.12) | copy-start | bytes 12292
  100.1 2.0 %copy-start.23 = (f32[8,8,64,64]{2,3,1,0:T(8,128)S(1)}, f32[8,8,64,64]{2,3,1,0:T(8,128)}, u32[]{:S(2)}) copy-start(f32[8,8,64,64]{2,3,1,0:T(8,128)} %get-tuple-element.15) | copy-start | bytes 3145732
  107.7 3.8 %copy-start.14 = (bf16[8,64,1,8,64]{1,4,3,0,2:T(8,128)(2,1)S(1)}, bf16[8,64,1,8,64]{1,4,3,0,2:T(8,128)(2,1)}, u32[]{:S(2)}) copy-start(bf16[8,64,1,8,64]{1,4,3,0,2:T(8,128)(2,1)} %fusion.20) | copy-start | bytes 1572868
  110.7 1.2 copy-start.12
  110.7 1.5 copy-start.13
  124.8 1.7 copy-start.21
  124.8 2.4 %copy-start.22 = (bf16[1024,1536]{1,0:T(8,128)(2,1)S(1)}, bf16[1024,1536]{1,0:T(8,128)(2,1)}, u32[]{:S(2)}) copy-start(bf16[1024,1536]{1,0:T(8,128)(2,1)} %param.13) | copy-start | bytes 9437188
  127.2 1.9 %copy-start.10 = (bf16[1,16,32,1024]{3,2,1,0:T(8,128)(2,1)S(1)}, bf16[1,16,32,1024]{3,2,1,0:T(8,128)(2,1)}, u32[]{:S(2)}) copy-start(bf16[1,16,32,1024]{3,2,1,0:T(8,128)(2,1)} %multiply_convert_fusion) | copy-start | bytes 3145732
  131.5 1.2 copy-start.15
  131.6 39.5 %collective-permute-start.2 = (bf16[2,4,32,1024]{3,2,1,0:T(8,128)(2,1)S(1)}, bf16[2,4,32,1024]{3,2,1,0:T(8,128)(2,1)S(1)}, u32[]{:S(2)}, u32[]{:S(2)}) collective-permute-start(bf16[2,4,32,1024]{3,2,1,0:T(8,128)(2,1)S(1)} %pad_maximum_fusion.5), channel_id=1, source_target_pairs={{0,16},{16,32},{32,48},{48,64},{64,80},{80,96},{96,112},{112,128},... | collective-permute-start | bytes 1572872 | tf_op jit(solution)/shard_map/ppermute | solution.py:22
  171.3 7.3 %collective-permute-start.3 = (bf16[2,16,4,1024]{3,2,1,0:T(4,128)(2,1)S(1)}, bf16[2,16,4,1024]{3,2,1,0:T(4,128)(2,1)S(1)}, u32[]{:S(2)}, u32[]{:S(2)}) collective-permute-start(bf16[2,16,4,1024]{3,2,1,0:T(4,128)(2,1)S(1)} %pad_maximum_fusion.6), channel_id=1, source_target_pairs={{0,4},{4,8},{8,12},{12,0},{1,5},{5,9},{9,13},{13,1},{2,6},{6,10},{... | collective-permute-start | bytes 786440 | tf_op jit(solution)/shard_map/ppermute | solution.py:22
  176.4 3.1 %copy-start.5 = (bf16[1,16,32,1024]{3,2,1,0:T(8,128)(2,1)S(1)}, bf16[1,16,32,1024]{3,2,1,0:T(8,128)(2,1)}, u32[]{:S(2)}) copy-start(bf16[1,16,32,1024]{3,2,1,0:T(8,128)(2,1)} %param.11) | copy-start | bytes 3145732
  176.4 3.1 %copy-start.6 = (bf16[1,16,32,1024]{3,2,1,0:T(8,128)(2,1)S(1)}, bf16[1,16,32,1024]{3,2,1,0:T(8,128)(2,1)}, u32[]{:S(2)}) copy-start(bf16[1,16,32,1024]{3,2,1,0:T(8,128)(2,1)} %param.10) | copy-start | bytes 3145732

commit v2 on v1

--- a/solution.py
+++ b/solution.py
@@ -9,10 +9,7 @@
 from jax.sharding import PartitionSpec as P
 
 MESH = pl.DeviceIdType.MESH
-
 SHIFT = 4
-
-
 EPS = 1e-06
 
 
@@ -22,128 +19,189 @@
     return lax.ppermute(value, axis, pairs)
 
 
-def offset_tables(window):
-    position = np.arange(window * window)
-    row_pos = position // window
-    col_pos = position % window
-    row_offset = row_pos[:, None] - row_pos[None, :] + window - 1
-    col_offset = col_pos[:, None] - col_pos[None, :] + window - 1
-    return (row_offset, col_offset)
-
-
-def to_windows(tokens, window):
-    rows_n, cols_n, chans = tokens.shape
-    blocks = tokens.reshape(rows_n // window, window, cols_n // window, window, chans)
-    return blocks.transpose(0, 2, 1, 3, 4).reshape(-1, window * window, chans)
-
-
-def from_windows(blocks, rows_n, cols_n, window):
-    chans = blocks.shape[-1]
-    grid = blocks.reshape(rows_n // window, cols_n // window, window, window, chans)
-    return grid.transpose(0, 2, 1, 3, 4).reshape(rows_n, cols_n, chans)
-
-
-def contract(left, right, left_dim, right_dim):
-    return lax.dot_general(
-        left, right, (((left_dim,), (right_dim,)), ((), ())), preferred_element_type=jnp.float32
-    )
-
-
-def window_block(shifted, grad_shifted, gain, w_qkv, w_out, bias_table):
-    f32 = jnp.float32
-    bf16 = jnp.bfloat16
-    rows_n, cols_n, features = shifted.shape
-    head_count = bias_table.shape[0]
-    window = (bias_table.shape[1] + 1) // 2
+def to_blocks(tile):
+    rows, cols, features = tile.shape
+    blocks = tile.reshape(rows // 4, 4, cols // 4, 4, features)
+    return blocks.transpose(0, 2, 1, 3, 4).reshape(rows // 4, cols // 4, 16, features)
+
+
+def from_blocks(blocks):
+    brows, bcols, _, features = blocks.shape
+    tile = blocks.reshape(brows, bcols, 4, 4, features).transpose(0, 2, 1, 3, 4)
+    return tile.reshape(brows * 4, bcols * 4, features)
+
+
+def pull(paired):
+    rim = passed_along(paired[:, :1], "rows", -1)
+    paired = jnp.concatenate([paired[:, 1:], rim], axis=1)
+    rim = passed_along(paired[:, :, :1], "cols", -1)
+    return jnp.concatenate([paired[:, :, 1:], rim], axis=2)
+
+
+def push(paired):
+    rim = passed_along(paired[:, -1:], "rows", 1)
+    paired = jnp.concatenate([rim, paired[:, :-1]], axis=1)
+    rim = passed_along(paired[:, :, -1:], "cols", 1)
+    return jnp.concatenate([rim, paired[:, :, :-1]], axis=2)
+
+
+def windows(blocks):
+    brows, bcols, size, features = blocks.shape
+    value = blocks.reshape(brows // 2, 2, bcols // 2, 2, size, features)
+    return value.transpose(0, 2, 1, 3, 4, 5).reshape(brows * bcols * size, features)
+
+
+def unwindows(tokens, brows, bcols):
+    value = tokens.reshape(brows // 2, bcols // 2, 2, 2, 16, tokens.shape[-1])
+    return value.transpose(0, 2, 1, 3, 4, 5).reshape(brows, bcols, 16, tokens.shape[-1])
+
+
+def token_place(index):
+    return (index // 32) * 4 + (index % 16) // 4, ((index // 16) % 2) * 4 + index % 4
+
+
+def nt(left, right):
+    return lax.dot_general(left, right, (((1,), (1,)), ((), ())), preferred_element_type=jnp.float32)
+
+
+def tn(left, right):
+    return lax.dot_general(left, right, (((0,), (0,)), ((), ())), preferred_element_type=jnp.float32)
+
+
+def block_kernel(x_ref, g_ref, gain_ref, wqkv_ref, wout_ref, table_ref,
+                 att_ref, gtok_ref, part_ref,
+                 norm_t, g_t, inv_ref, proj, gheads, heads, gproj, bias_ref):
+    f32, bf16 = jnp.float32, jnp.bfloat16
+    i32 = jnp.int32
+    tokens, features = x_ref.shape
+    head_dim, group = 64, 256
+    all_heads = wout_ref.shape[0]
+    scale = head_dim ** -0.5
+    rows = 128
+
+    krow, kcol = token_place(lax.broadcasted_iota(i32, (64, 128), 0))
+    qrow, qcol = token_place(lax.broadcasted_iota(i32, (64, 128), 1) % 64)
+    offset = (qrow - krow + 7) * 16 + qcol - kcol + 7
+    low, low_half = offset % 128, offset < 128
+    first_head = lax.broadcasted_iota(i32, (64, 128), 1) < 64
+
+    def bias_of(head):
+        a = jnp.broadcast_to(table_ref[head:head + 1, 0:128], (64, 128))
+        b = jnp.broadcast_to(table_ref[head:head + 1, 128:256], (64, 128))
+        at = functools.partial(jnp.take_along_axis, indices=low, axis=1, mode="promise_in_bounds")
+        return jnp.where(low_half, at(a), at(b))
+
+    for duo in range(all_heads // 128):
+        bias_ref[duo // 2, :, (duo % 2) * 128:(duo % 2) * 128 + 128] = jnp.where(
+            first_head, bias_of(2 * duo), bias_of(2 * duo + 1))
+
+    def project(step, carry):
+        part = pl.ds(pl.multiple_of(step * rows, rows), rows)
+        value = x_ref[part, :].astype(f32)
+        inverse = lax.rsqrt(jnp.mean(value * value, axis=1, keepdims=True) + EPS)
+        inv_ref[part, :] = inverse
+        normed = (value * inverse * gain_ref[...]).astype(bf16)
+        upstream = g_ref[part, :]
+        norm_t[step] = normed.T
+        g_t[step] = upstream.T
+        proj[part, :] = jnp.dot(normed, wqkv_ref[...], preferred_element_type=f32).astype(bf16)
+        gheads[part, :] = nt(upstream, wout_ref[...]).astype(bf16)
+        return carry
+
+    lax.fori_loop(0, tokens // rows, project, 0)
+
+    head_row = lax.broadcasted_iota(i32, (group, group), 0) // head_dim
+    head_lane = lax.broadcasted_iota(i32, (group, group), 1) // head_dim
+    diagonal = head_row == head_lane
+    lane64 = lax.broadcasted_iota(i32, (64, group), 1) // head_dim
+
+    def spread(value):
+        return jnp.where(diagonal, jnp.concatenate([value] * 4, axis=0), jnp.zeros((), value.dtype))
+
+    def gather_heads(full):
+        out = full[0:64]
+        for h in range(1, 4):
+            out = jnp.where(lane64 == h, full[h * 64:h * 64 + 64], out)
+        return out
+
+    def attend(win, carry):
+        part = pl.ds(pl.multiple_of(win * 64, 64), 64)
+        for grp in range(all_heads // group):
+            lo = grp * group
+            q = proj[part, lo:lo + group]
+            k = proj[part, all_heads + lo:all_heads + lo + group]
+            v = proj[part, 2 * all_heads + lo:2 * all_heads + lo + group]
+            go = gheads[part, lo:lo + group]
+            q_wide, go_wide = spread(q), spread(go)
+            scores = nt(k, q_wide) * scale + bias_ref[grp]
+            expo = jnp.exp(scores - jnp.max(scores, axis=0, keepdims=True))
+            soft = expo * (1.0 / jnp.sum(expo, axis=0, keepdims=True))
+            soft_b = soft.astype(bf16)
+            gp = nt(v, go_wide)
+            inner = jnp.sum(gp * soft, axis=0, keepdims=True)
+            gs = (soft * (gp - inner) * scale).astype(bf16)
+            heads[part, lo:lo + group] = gather_heads(tn(soft_b, v)).astype(bf16)
+            gproj[part, lo:lo + group] = gather_heads(tn(gs, k)).astype(bf16)
+            gproj[part, all_heads + lo:all_heads + lo + group] = jnp.dot(
+                gs, q_wide, preferred_element_type=f32).astype(bf16)
+            gproj[part, 2 * all_heads + lo:2 * all_heads + lo + group] = jnp.dot(
+                soft_b, go_wide, preferred_element_type=f32).astype(bf16)
+        return carry
+
+    lax.fori_loop(0, tokens // 64, attend, 0)
+
+    def weights(step, carry):
+        part = pl.ds(pl.multiple_of(step * rows, rows), rows)
+        left = jnp.concatenate([norm_t[t, part, :] for t in range(tokens // rows)], axis=1)
+        part_ref[part, 0:3 * all_heads] = jnp.dot(left, gproj[...], preferred_element_type=f32).astype(bf16)
+        left = jnp.concatenate([g_t[t, part, :] for t in range(tokens // rows)], axis=1)
+        part_ref[part, 3 * all_heads:] = jnp.dot(left, heads[...], preferred_element_type=f32).astype(bf16)
+        return carry
+
+    lax.fori_loop(0, features // rows, weights, 0)
+
+    def finish(step, carry):
+        part = pl.ds(pl.multiple_of(step * rows, rows), rows)
+        att_ref[part, :] = jnp.dot(heads[part, :], wout_ref[...], preferred_element_type=f32).astype(bf16)
+        grad_normed = nt(gproj[part, :], wqkv_ref[...])
+        inverse = inv_ref[part, :]
+        unit = x_ref[part, :].astype(f32) * inverse
+        grad_unit = grad_normed * gain_ref[...]
+        mean = jnp.mean(grad_unit * unit, axis=1, keepdims=True)
+        gtok_ref[part, :] = (inverse * (grad_unit - unit * mean)).astype(bf16)
+        return carry
+
+    lax.fori_loop(0, tokens // rows, finish, 0)
+
+
+def window_block(x, g, gain, w_qkv, w_out, bias_table):
+    f32, bf16 = jnp.float32, jnp.bfloat16
+    tokens, features = x.shape
     all_heads = w_out.shape[0]
-    head_size = all_heads // head_count
-    score_scale = head_size ** (-0.5)
-    flat_rows = shifted.reshape(rows_n * cols_n, features).astype(f32)
-    inverse = lax.rsqrt(jnp.mean(flat_rows * flat_rows, axis=1, keepdims=True) + EPS)
-    unit_rows = flat_rows * inverse
-    normed = (unit_rows * gain).astype(bf16)
-    projected = jnp.dot(normed, w_qkv, preferred_element_type=f32).astype(bf16)
-    win_proj = to_windows(projected.reshape(rows_n, cols_n, 3 * all_heads), window)
-    count_win = win_proj.shape[0]
-    win_proj = win_proj.reshape(count_win, window * window, 3, head_count, head_size)
-    queries = win_proj[:, :, 0]
-    keys_win = win_proj[:, :, 1]
-    values_win = win_proj[:, :, 2]
-    row_offset, col_offset = offset_tables(window)
-    bias = bias_table[:, row_offset, col_offset]
-    scores = (
-        jnp.einsum("nqhe,nkhe->nhqk", queries, keys_win, preferred_element_type=f32) * score_scale
-        + bias[None]
-    )
-    peak = jnp.max(scores, axis=-1, keepdims=True)
-    expo = jnp.exp(scores - peak)
-    softmax_f = expo / jnp.sum(expo, axis=-1, keepdims=True)
-    softmax_b = softmax_f.astype(bf16)
-    heads_win = jnp.einsum(
-        "nhqk,nkhe->nqhe", softmax_b, values_win, preferred_element_type=f32
-    ).astype(bf16)
-    heads_out = from_windows(
-        heads_win.reshape(count_win, window * window, all_heads), rows_n, cols_n, window
-    )
-    heads_out = heads_out.reshape(rows_n * cols_n, all_heads)
-    attention = jnp.dot(heads_out, w_out, preferred_element_type=f32).astype(bf16)
-    upstream = grad_shifted.reshape(rows_n * cols_n, features)
-    part_out_t = contract(upstream, heads_out, 0, 0)
-    grad_heads = contract(upstream, w_out, 1, 1).astype(bf16)
-    grad_win = to_windows(grad_heads.reshape(rows_n, cols_n, all_heads), window)
-    grad_win = grad_win.reshape(count_win, window * window, head_count, head_size)
-    grad_probs = jnp.einsum("nqhe,nkhe->nhqk", grad_win, values_win, preferred_element_type=f32)
-    grad_values = jnp.einsum(
-        "nhqk,nqhe->nkhe", softmax_b, grad_win, preferred_element_type=f32
-    ).astype(bf16)
-    inner = jnp.sum(grad_probs * softmax_f, axis=-1, keepdims=True)
-    grad_scores = (softmax_f * (grad_probs - inner) * score_scale).astype(bf16)
-    grad_queries = jnp.einsum(
-        "nhqk,nkhe->nqhe", grad_scores, keys_win, preferred_element_type=f32
-    ).astype(bf16)
-    grad_keys = jnp.einsum(
-        "nhqk,nqhe->nkhe", grad_scores, queries, preferred_element_type=f32
-    ).astype(bf16)
-    grad_projected = jnp.stack([grad_queries, grad_keys, grad_values], axis=2)
-    grad_projected = grad_projected.reshape(count_win, window * window, 3 * all_heads)
-    grad_projected = from_windows(grad_projected, rows_n, cols_n, window).reshape(
-        rows_n * cols_n, 3 * all_heads
-    )
-    part_qkv = contract(normed, grad_projected, 0, 0)
-    grad_normed = contract(grad_projected, w_qkv, 1, 1)
-    part_gain = jnp.sum(grad_normed * unit_rows, axis=0)
-    grad_unit = grad_normed * gain
-    grad_tokens = inverse * (
-        grad_unit - unit_rows * jnp.mean(grad_unit * unit_rows, axis=1, keepdims=True)
-    )
-    grad_tokens = grad_tokens.astype(bf16)
-    return (
-        attention.reshape(rows_n, cols_n, features),
-        grad_tokens.reshape(rows_n, cols_n, features),
-        part_qkv,
-        part_out_t,
-        part_gain,
-    )
-
-
-def pull_rows(paired):
-    rim_rows = passed_along(paired[:, :SHIFT], "rows", -1)
-    return jnp.concatenate([paired[:, SHIFT:], rim_rows], axis=1)
-
-
-def pull_cols(paired):
-    rim_cols = passed_along(paired[:, :, :SHIFT], "cols", -1)
-    return jnp.concatenate([paired[:, :, SHIFT:], rim_cols], axis=2)
-
-
-def push_rows(paired):
-    rim_rows = passed_along(paired[:, -SHIFT:], "rows", 1)
-    return jnp.concatenate([rim_rows, paired[:, :-SHIFT]], axis=1)
-
-
-def push_cols(paired):
-    rim_cols = passed_along(paired[:, :, -SHIFT:], "cols", 1)
-    return jnp.concatenate([rim_cols, paired[:, :, :-SHIFT]], axis=2)
+    table = jnp.pad(bias_table, ((0, 0), (0, 1), (0, 1))).reshape(bias_table.shape[0], 256)
+    vmem = pl.BlockSpec(memory_space=pltpu.VMEM)
+    return pl.pallas_call(
+        block_kernel,
+        out_shape=(
+            jax.ShapeDtypeStruct((tokens, features), bf16),
+            jax.ShapeDtypeStruct((tokens, features), bf16),
+            jax.ShapeDtypeStruct((features, 4 * all_heads), bf16),
+        ),
+        in_specs=[vmem] * 6,
+        out_specs=(vmem,) * 3,
+        scratch_shapes=[
+            pltpu.VMEM((tokens // 128, features, 128), bf16),
+            pltpu.VMEM((tokens // 128, features, 128), bf16),
+            pltpu.VMEM((tokens, 1), f32),
+            pltpu.VMEM((tokens, 3 * all_heads), bf16),
+            pltpu.VMEM((tokens, all_heads), bf16),
+            pltpu.VMEM((tokens, all_heads), bf16),
+            pltpu.VMEM((tokens, 3 * all_heads), bf16),
+            pltpu.VMEM((2, 64, 256), f32),
+        ],
+        compiler_params=pltpu.CompilerParams(vmem_limit_bytes=48 * 1024 * 1024),
+        name="window_block",
+    )(x, g, gain.reshape(1, features), w_qkv, w_out, table)
 
 
 def rs_kernel(nz, nx, m_ref, out_ref, recv0, acc_x, acc_y, acc_z,
@@ -331,16 +389,15 @@
 
 def local(image, cotangent, gain, w_qkv, w_out, bias_table):
     f32 = jnp.float32
-    paired = jnp.stack([image[0], cotangent[0]])
-    shifted = pull_cols(pull_rows(paired))
-    attention, grad_tokens, part_qkv, part_out_t, part_gain = window_block(
-        shifted[0], shifted[1], gain, w_qkv, w_out, bias_table
+    blocks = jnp.stack([to_blocks(image[0]), to_blocks(cotangent[0])])
+    shifted = pull(blocks)
+    attention, grad_tokens, partial = window_block(
+        windows(shifted[0]), windows(shifted[1]), gain, w_qkv, w_out, bias_table
     )
-    branch = jnp.stack([attention, grad_tokens])
-    returned = push_cols(push_rows(branch))
-    result = (image[0].astype(f32) + returned[0].astype(f32)).astype(jnp.bfloat16)
-    grad_result = (cotangent[0].astype(f32) + returned[1].astype(f32)).astype(jnp.bfloat16)
-    partial = jnp.concatenate([part_qkv.astype(jnp.bfloat16), part_out_t.astype(jnp.bfloat16)], axis=1)
+    brows, bcols = blocks.shape[1:3]
+    returned = push(jnp.stack([unwindows(attention, brows, bcols), unwindows(grad_tokens, brows, bcols)]))
+    result = (image[0].astype(f32) + from_blocks(returned[0]).astype(f32)).astype(jnp.bfloat16)
+    grad_result = (cotangent[0].astype(f32) + from_blocks(returned[1]).astype(f32)).astype(jnp.bfloat16)
     summed = reduce_scatter(partial, lax.axis_size("rows") // 2, lax.axis_size("rep"))
     total_count = (
         lax.axis_size("rows")

time: 184 us -> 126 us (0.68)
  local copies, waits for them, and re-layouts: 65.4 us -> 18.4 us
  matrix products: 35 us -> 0 us
  Pallas kernels: 37 us -> 61.5 us
  waiting for transfers between devices: 12.5 us -> 19.2 us
  other arithmetic: 16.3 us -> 11.1 us
    dot_general x11 -> x0, matrix products: 31.4 us -> none  [the longest x4 7.53 us: contract(): lax.dot_general(left, right, (((left_dim,), (right_dim,)), ((), ())), pre...]
    gather x2 -> x0, local copies, waits for them, and re-layouts: 27.4 us -> none  [window_block(): bias = bias_table[:, row_offset, col_offset]]
    pallas_call x0 -> x1, Pallas kernels: none -> 24.1 us  [window_block(): pl.pallas_call(block_kernel, out_shape=(jax.ShapeDtypeStruct((tokens, fea...]
    another operation x9 -> x2, local copies, waits for them, and re-layouts: 22.1 us -> 1.98 us  [to_blocks(): blocks = tile.reshape(rows // 4, 4, cols // 4, 4, features)]
    convert_element_type x1 -> x6, local copies, waits for them, and re-layouts: 1.69 us -> 11.3 us  [the longest x3 6.91 us: local(): from_blocks(returned[1]).astype(f32)]
    ppermute x4, waiting for transfers between devices: 12.5 us -> 19.2 us  [passed_along(): return lax.ppermute(value, axis, pairs)]
    unnamed x51 -> x13, local copies, waits for them, and re-layouts: 7.47 us -> 2.73 us
    sub x1 -> x0, matrix products: 3.67 us -> none  [window_block(): expo = jnp.exp(scores - peak)]
  transfers between devices with their start and end apart: 4 -> 4, of which waited for: 2 -> 3; matrix products, arithmetic and copies ran while one was open for 18% -> 3% of each run, Pallas kernels for 0% -> 0%
where the time goes in v2:
time: 126 us; the launch traced here: 125 us
  Pallas kernels  61.5 us (49%)
  waiting for transfers between devices  19.2 us (15%)
  local copies, waits for them, and re-layouts  18.4 us (15%)
  starting transfers between devices  13.7 us (11%)
  other arithmetic  11.1 us (9%)
    pallas_call x1, Pallas kernels, reduce_scatter(): pl.pallas_call(functools.partial(rs_kernel, nz, nx), out_shape=jax.ShapeD...  37.4 us
    pallas_call x1, Pallas kernels, window_block(): pl.pallas_call(block_kernel, out_shape=(jax.ShapeDtypeStruct((tokens, fea...  24.1 us
    ppermute x4, waiting for transfers between devices, passed_along(): return lax.ppermute(value, axis, pairs)  19.2 us
    ppermute x4, starting transfers between devices, passed_along(): return lax.ppermute(value, axis, pairs)  13.7 us
    convert_element_type x3, local copies, waits for them, and re-layouts, local(): from_blocks(returned[1]).astype(f32)  6.91 us
    convert_element_type x1, other arithmetic, local(): (cotangent[0].astype(f32) + from_blocks(returned[1]).astype(f32)).astype(...  4.59 us
    convert_element_type x3, local copies, waits for them, and re-layouts, local(): from_blocks(returned[0]).astype(f32)  4.38 us
    unnamed x13, local copies, waits for them, and re-layouts  2.73 us
  transfers between devices with their start and end apart: 4, of which 3 were waited for; matrix products, arithmetic and copies ran while one was open for 3% of the time, Pallas kernels for 0%

profile of v2, /device:TPU:1, one launch (start us, length us, event | category | flops | bytes accessed | tf_op | source)
XLA Modules:
  0.0 124.7 jit_solution(3429168222308700010)
XLA Ops:
  0.6 1.5 %reshape_squeeze.14 = bf16[4,4,8,4,1024]{4,3,2,1,0:T(4,128)(2,1)S(1)} reshape(bf16[1,16,32,1024]{3,2,1,0:T(8,128)(2,1)} %param.6) | data formatting | bytes 2097152 | tf_op jit(solution)/shard_map/reshape;squeeze | solution.py:24
  2.2 0.4 copy.21
  2.6 0.4 reshape_squeeze.15
  3.0 0.4 copy.22
  3.5 9.1 %collective-permute-start = (bf16[2,1,8,16,1024]{4,2,3,1,0:T(8,128)(2,1)S(1)}, bf16[2,1,8,16,1024]{4,2,3,1,0:T(8,128)(2,1)S(1)}, u32[]{:S(2)}, u32[]{:S(2)}) collective-permute-start(bf16[2,1,8,16,1024]{4,2,3,1,0:T(8,128)(2,1)S(1)} %pad_maximum_fusion.5), channel_id=1, source_target_pairs={{0,240},{16,0},{32,16},{48,32},{64,48},{80,64},{96,80},{112,96},{1... | collective-permute-start | bytes 1572872 | tf_op jit(solution)/shard_map/ppermute | solution.py:19
  12.6 0.1 fusion.1
  12.7 10.4 %collective-permute-done = bf16[2,1,8,16,1024]{4,2,3,1,0:T(8,128)(2,1)S(1)} collective-permute-done((bf16[2,1,8,16,1024]{4,2,3,1,0:T(8,128)(2,1)S(1)}, bf16[2,1,8,16,1024]{4,2,3,1,0:T(8,128)(2,1)S(1)}, u32[]{:S(2)}, u32[]{:S(2)}) %collective-permute-start) | collective-permute-done | bytes 524320 | tf_op jit(solution)/shard_map/ppermute | solution.py:19
  23.2 1.2 pad_maximum_fusion.4
  24.4 1.5 %collective-permute-start.1 = (bf16[2,4,1,16,1024]{4,2,3,1,0:T(2,128)(2,1)}, bf16[2,4,1,16,1024]{4,2,3,1,0:T(2,128)(2,1)S(1)}, u32[]{:S(2)}, u32[]{:S(2)}) collective-permute-start(bf16[2,4,1,16,1024]{4,2,3,1,0:T(2,128)(2,1)} %pad_maximum_fusion.4), channel_id=1, source_target_pairs={{0,12},{4,0},{8,4},{12,8},{1,13},{5,1},{9,5},{13,9},{2,14},{6,2},{... | collective-permute-start | bytes 786440 | tf_op jit(solution)/shard_map/ppermute | solution.py:19
  26.0 0.6 slice_maximum_fusion
  26.6 6.7 %collective-permute-done.1 = bf16[2,4,1,16,1024]{4,2,3,1,0:T(2,128)(2,1)S(1)} collective-permute-done((bf16[2,4,1,16,1024]{4,2,3,1,0:T(2,128)(2,1)}, bf16[2,4,1,16,1024]{4,2,3,1,0:T(2,128)(2,1)S(1)}, u32[]{:S(2)}, u32[]{:S(2)}) %collective-permute-start.1) | collective-permute-done | bytes 262176 | tf_op jit(solution)/shard_map/ppermute | solution.py:19
  33.3 1.1 pad_maximum_fusion.2
  34.4 0.6 copy.25
  35.1 0.6 copy.23
  35.8 0.5 copy-done.1
  36.3 24.1 %window_block.1 = (bf16[512,1024]{1,0:T(8,128)(2,1)S(1)}, bf16[512,1024]{1,0:T(8,128)(2,1)S(1)}, bf16[1024,2048]{1,0:T(8,128)(2,1)}) custom-call(bf16[512,1024]{1,0:T(8,128)(2,1)S(1)} %bitcast.36, bf16[512,1024]{1,0:T(8,128)(2,1)S(1)} %bitcast.35, f32[1,1024]{1,0:T(1,128)S(1)} %bitcast.39, bf16[1024,1536]{1,0:T(8,128)(2,1)} %wqkv_ref.1, ...), custom_call_target="tpu_custom_call" | custom-call | tf_op jit(solution)/shard_map/window_block/pallas_call | solution.py:183
  60.7 2.2 %copy-done = bf16[1024,2048]{1,0:T(8,128)(2,1)S(1)} copy-done((bf16[1024,2048]{1,0:T(8,128)(2,1)S(1)}, bf16[1024,2048]{1,0:T(8,128)(2,1)}, u32[]{:S(2)}) %copy-start) | copy-done | bytes 4194328
  62.9 37.4 %reduce_scatter.1 = f32[4,2048]{1,0:T(4,128)S(1)} custom-call(bf16[2,8,2,2,16,2048]{5,4,3,2,1,0:T(8,128)(2,1)S(1)} %bitcast.34), custom_call_target="tpu_custom_call" | custom-call | tf_op jit(solution)/shard_map/reduce_scatter/pallas_call | solution.py:377
  100.3 1.5 %multiply_reduce_fusion = (f32[4]{0:T(128)S(1)}, f32[4,1536]{1,0:T(4,128)}) fusion(bf16[1024,1536]{1,0:T(8,128)(2,1)} %wqkv_ref.1, s32[]{:T(128)S(6)} %select_n.4, f32[4,2048]{1,0:T(4,128)S(1)} %reduce_scatter.1), kind=kLoop, calls=%fused_computation.19 | loop fusion | flops 24572 | bytes 61460 | tf_op jit(solution)/shard_map/reduce_sum | solution.py:414
  101.8 2.9 %collective-permute-start.3 = (bf16[2,4,1,16,1024]{4,3,2,1,0:T(8,128)(2,1)S(1)}, bf16[2,4,1,16,1024]{4,3,2,1,0:T(8,128)(2,1)S(1)}, u32[]{:S(2)}, u32[]{:S(2)}) collective-permute-start(bf16[2,4,1,16,1024]{4,3,2,1,0:T(8,128)(2,1)S(1)} %pad_maximum_fusion.6), channel_id=1, source_target_pairs={{0,4},{4,8},{8,12},{12,0},{1,5},{5,9},{9,13},{13,1},{2,6},{6,10},{... | collective-permute-start | bytes 786440 | tf_op jit(solution)/shard_map/ppermute | solution.py:19
  104.7 0.6 dynamic-slice_divide_fusion
  105.3 0.6 multiply_bitcast_fusion
  105.9 2.1 %collective-permute-done.3 = bf16[2,4,1,16,1024]{4,3,2,1,0:T(8,128)(2,1)S(1)} collective-permute-done((bf16[2,4,1,16,1024]{4,3,2,1,0:T(8,128)(2,1)S(1)}, bf16[2,4,1,16,1024]{4,3,2,1,0:T(8,128)(2,1)S(1)}, u32[]{:S(2)}, u32[]{:S(2)}) %collective-permute-start.3) | collective-permute-done | bytes 262176 | tf_op jit(solution)/shard_map/ppermute | solution.py:19
  108.1 0.3 fusion
  108.3 0.4 slice_convert_fusion
  108.8 1.2 copy.32
  110.0 2.7 %copy.33 = f32[4,4,8,4,1024]{4,3,2,1,0:T(4,128)} copy(f32[4,4,8,4,1024]{4,2,3,1,0:T(8,128)S(1)} %bitcast.50) | data formatting | bytes 4194304 | tf_op jit(solution)/shard_map/convert_element_type | solution.py:400
  112.7 3.0 %reshape.69 = f32[1,16,32,1024]{3,2,1,0:T(8,128)} reshape(f32[4,4,8,4,1024]{4,3,2,1,0:T(4,128)} %copy.33) | data formatting | bytes 4194304 | tf_op jit(solution)/shard_map/convert_element_type | solution.py:400
  115.7 1.2 copy.30
  116.9 1.4 %copy.31 = f32[4,4,8,4,1024]{4,3,2,1,0:T(4,128)S(1)} copy(f32[4,4,8,4,1024]{4,2,3,1,0:T(8,128)S(1)} %bitcast.51) | data formatting | bytes 4194304 | tf_op jit(solution)/shard_map/convert_element_type | solution.py:399
  118.3 1.8 %reshape.68 = f32[1,16,32,1024]{3,2,1,0:T(8,128)} reshape(f32[4,4,8,4,1024]{4,3,2,1,0:T(4,128)S(1)} %copy.31) | data formatting | bytes 4194304 | tf_op jit(solution)/shard_map/convert_element_type | solution.py:399
  120.1 4.6 %add_convert_fusion = (bf16[1,16,32,1024]{3,2,1,0:T(8,128)(2,1)}, bf16[1,16,32,1024]{3,2,1,0:T(8,128)(2,1)}) fusion(f32[1,16,32,1024]{3,2,1,0:T(8,128)} %reshape.69, bf16[1,16,32,1024]{3,2,1,0:T(8,128)(2,1)S(1)} %copy-done.4, f32[1,16,32,1024]{3,2,1,0:T(8,128)} %reshape.68, bf16[1,16,32,1024]{3,2,1,0:T(8,128)(2,1)} %param.6), kind=kLoop, calls=%fused_computation.8 | loop fusion | flops 3145728 | bytes 8388608 | tf_op jit(solution)/shard_map/convert_element_type | solution.py:400
  (22 shorter events, 0.7 us)
Async XLA Ops:
  0.6 2.0 %copy-start.3 = (bf16[1,16,32,1024]{3,2,1,0:T(8,128)(2,1)S(1)}, bf16[1,16,32,1024]{3,2,1,0:T(8,128)(2,1)}, u32[]{:S(2)}) copy-start(bf16[1,16,32,1024]{3,2,1,0:T(8,128)(2,1)} %param.7) | copy-start | bytes 3145732
  3.5 19.7 %collective-permute-start = (bf16[2,1,8,16,1024]{4,2,3,1,0:T(8,128)(2,1)S(1)}, bf16[2,1,8,16,1024]{4,2,3,1,0:T(8,128)(2,1)S(1)}, u32[]{:S(2)}, u32[]{:S(2)}) collective-permute-start(bf16[2,1,8,16,1024]{4,2,3,1,0:T(8,128)(2,1)S(1)} %pad_maximum_fusion.5), channel_id=1, source_target_pairs={{0,240},{16,0},{32,16},{48,32},{64,48},{80,64},{96,80},{112,96},{1... | collective-permute-start | bytes 1572872 | tf_op jit(solution)/shard_map/ppermute | solution.py:19
  12.7 13.2 %copy-start.5 = (f32[8,15,15]{2,0,1:T(8,128)S(1)}, f32[8,15,15]{2,0,1:T(8,128)}, u32[]{:S(2)}) copy-start(f32[8,15,15]{2,0,1:T(8,128)} %param.11) | copy-start | bytes 21604
  24.4 8.9 %collective-permute-start.1 = (bf16[2,4,1,16,1024]{4,2,3,1,0:T(2,128)(2,1)}, bf16[2,4,1,16,1024]{4,2,3,1,0:T(2,128)(2,1)S(1)}, u32[]{:S(2)}, u32[]{:S(2)}) collective-permute-start(bf16[2,4,1,16,1024]{4,2,3,1,0:T(2,128)(2,1)} %pad_maximum_fusion.4), channel_id=1, source_target_pairs={{0,12},{4,0},{8,4},{12,8},{1,13},{5,1},{9,5},{13,9},{2,14},{6,2},{... | collective-permute-start | bytes 786440 | tf_op jit(solution)/shard_map/ppermute | solution.py:19
  35.1 1.2 copy-start.1
  35.1 1.2 copy-start.2
  60.6 41.1 %collective-permute-start.2 = (bf16[2,1,8,16,1024]{4,3,2,1,0:T(8,128)(2,1)S(1)}, bf16[2,1,8,16,1024]{4,3,2,1,0:T(8,128)(2,1)S(1)}, u32[]{:S(2)}, u32[]{:S(2)}) collective-permute-start(bf16[2,1,8,16,1024]{4,3,2,1,0:T(8,128)(2,1)S(1)} %pad_maximum_fusion.3), channel_id=1, source_target_pairs={{0,16},{16,32},{32,48},{48,64},{64,80},{80,96},{96,112},{112,128},... | collective-permute-start | bytes 1572872 | tf_op jit(solution)/shard_map/ppermute | solution.py:19
  60.7 2.2 %copy-start = (bf16[1024,2048]{1,0:T(8,128)(2,1)S(1)}, bf16[1024,2048]{1,0:T(8,128)(2,1)}, u32[]{:S(2)}) copy-start(bf16[1024,2048]{1,0:T(8,128)(2,1)} %get-tuple-element.10) | copy-start | bytes 12582916
  101.8 6.3 %collective-permute-start.3 = (bf16[2,4,1,16,1024]{4,3,2,1,0:T(8,128)(2,1)S(1)}, bf16[2,4,1,16,1024]{4,3,2,1,0:T(8,128)(2,1)S(1)}, u32[]{:S(2)}, u32[]{:S(2)}) collective-permute-start(bf16[2,4,1,16,1024]{4,3,2,1,0:T(8,128)(2,1)S(1)} %pad_maximum_fusion.6), channel_id=1, source_target_pairs={{0,4},{4,8},{8,12},{12,0},{1,5},{5,9},{9,13},{13,1},{2,6},{6,10},{... | collective-permute-start | bytes 786440 | tf_op jit(solution)/shard_map/ppermute | solution.py:19
  118.3 1.8 %copy-start.4 = (bf16[1,16,32,1024]{3,2,1,0:T(8,128)(2,1)S(1)}, bf16[1,16,32,1024]{3,2,1,0:T(8,128)(2,1)}, u32[]{:S(2)}) copy-start(bf16[1,16,32,1024]{3,2,1,0:T(8,128)(2,1)} %param.7) | copy-start | bytes 3145732

commit v3 on v0

v3 whole, which is shorter than its diff:
```python
import functools

import jax
import jax.numpy as jnp
import numpy as np
from jax import lax
from jax.experimental import pallas as pl
from jax.experimental.pallas import tpu as pltpu
from jax.sharding import PartitionSpec as P

MESH = pl.DeviceIdType.MESH
EPS = 1e-06
GROUP = 256
HEAD = 64
PARTS = (("zxy", 0, 0), ("xyz", 0, 512), ("yzx", 1, 0), ("xyz", 1, 512))


def token_place(index):
    return (index // 32) * 4 + (index % 16) // 4, ((index // 16) % 2) * 4 + index % 4


def nt(left, right):
    return lax.dot_general(left, right, (((1,), (1,)), ((), ())), preferred_element_type=jnp.float32)


def tn(left, right):
    return lax.dot_general(left, right, (((0,), (0,)), ((), ())), preferred_element_type=jnp.float32)


def nn(left, right):
    return jnp.dot(left, right, preferred_element_type=jnp.float32)


def block_place(rb, cb):
    if cb == 0:
        return ("corner", 0, 0) if rb == 3 else ("left", rb, 0)
    if rb in (1, 2):
        return ("window", 3, (rb - 1) * 2) if cb == 7 else ("window", (cb - 1) // 2, (rb - 1) * 2 + (cb - 1) % 2)
    if rb == 3:
        return ("window", 4 + (cb - 1) // 2, (cb - 1) % 2) if cb <= 4 else ("down", cb - 5, 0)
    if cb <= 4:
        return ("up", (cb - 1) // 2, (cb - 1) % 2)
    return ("window", 7, 2) if cb == 7 else ("window", 6, 2 + cb - 5)


def kernel(nz, nx, factor,
           img_ref, cot_ref, gain_ref, wqkv_hbm, wout_hbm, table_ref,
           out_ref, gimg_ref, gqkv_ref, gout_ref, ggain_ref,
           wqkv_ref, wout_ref, tok, ret,
           up, down, left, corner, b_up, b_down, b_left, b_corner,
           norm_t, g_t, inv_ref, proj, gheads, heads, gproj, bias_ref,
           m_ref, recv0, *rest):
    f32, bf16, i32 = jnp.float32, jnp.bfloat16, jnp.int32
    count_parts = len(PARTS)
    acc1, acc2, acc3 = rest[0:4], rest[4:8], rest[8:12]
    rx1, rx2, rx3 = rest[12:16], rest[16:20], rest[20:24]
    swap_out, swap_in, sends, recvs, local_sems = rest[24:]
    scale = HEAD ** -0.5
    all_heads = 2 * GROUP

    row, col, x = lax.axis_index("rows"), lax.axis_index("cols"), lax.axis_index("rep")
    yh, z = row // nz, row % nz
    yl, core = col // 2, col % 2
    y = yh * 2 + yl
    place = {"x": x, "y": y, "z": z}
    size = {"x": nx, "y": 4, "z": nz}
    pair = (row, yl * 2 + 1 - core, x)
    above = ((row + 2 * nz - 1) % (2 * nz), col, x)
    below = ((row + 1) % (2 * nz), col, x)
    lefty = (row, (col + 3) % 4, x)
    right = (row, (col + 1) % 4, x)
    below_left = ((row + 1) % (2 * nz), (col + 3) % 4, x)
    above_right = ((row + 2 * nz - 1) % (2 * nz), (col + 1) % 4, x)

    def on(axis, step):
        other = (place[axis] + step) % size[axis]
        if axis == "x":
            return other, (row, col, other)
        if axis == "y":
            return other, ((other // 2) * nz + z, (other % 2) * 2 + core, x)
        return other, (yh * nz + other, col, x)

    copies = [
        pltpu.make_async_copy(wqkv_hbm, wqkv_ref, local_sems.at[0]),
        pltpu.make_async_copy(wout_hbm, wout_ref, local_sems.at[1]),
    ]
    for copy in copies:
        copy.start()

    barrier = pltpu.get_barrier_semaphore()
    peers = [pair, above, below, lefty, right, below_left, above_right]
    for axis in "xyz":
        peers += [on(axis, step)[1] for step in range(1, size[axis])]
    for peer in peers:
        pl.semaphore_signal(barrier, inc=1, device_id=peer, device_id_type=MESH)

    slot = iter(range(1000))
    started = []

    def send(source, target, device):
        index = next(slot)
        copy = pltpu.make_async_remote_copy(
            src_ref=source, dst_ref=target, send_sem=sends.at[index], recv_sem=recvs.at[index],
            device_id=device, device_id_type=MESH)
        copy.start()
        started.append(copy)
        return copy

    def landed(arrivals):
        for copy in arrivals:
            copy.wait_recv()

    rim = {"up": up, "down": down, "left": left, "corner": corner}
    back = {"up": b_up, "down": b_down, "left": b_left, "corner": b_corner}
    one = lax.broadcasted_iota(i32, (128, 128), 0)
    two = lax.broadcasted_iota(i32, (128, 128), 1)
    to_block = (two == ((one % 16) // 4) * 32 + (one // 16) * 4 + one % 4).astype(bf16)
    from_block = (two == ((one % 32) // 4) * 16 + (one // 32) * 4 + one % 4).astype(bf16)

    def block_at(own, rims, which, spot):
        name, a, b = spot
        if name == "window":
            return own.at[which, a, b]
        return rims[name].at[which, a, b]

    for rb in (0, 3, 1, 2):
        for which, ref in ((0, img_ref), (1, cot_ref)):
            value = nn(to_block, ref[rb * 4:rb * 4 + 4].reshape(128, 1024)).astype(bf16)
            for cb in range(8):
                block_at(tok, rim, which, block_place(rb, cb))[...] = value[cb * 16:cb * 16 + 16]

    pl.semaphore_wait(barrier, len(peers))
    from_right = [
        send(left.at[:, 1, 0], tok.at[:, 3, 1], lefty),
        send(left.at[:, 2, 0], tok.at[:, 3, 3], lefty),
    ]
    from_below = [send(up, tok.at[:, 4:6, 2:4], above)]
    from_above = [
        send(down.at[:, 0, 0], tok.at[:, 6, 0], below),
        send(down.at[:, 1, 0], tok.at[:, 6, 1], below),
        send(down.at[:, 2, 0], tok.at[:, 7, 0], below),
        send(corner.at[:, 0, 0], tok.at[:, 7, 1], below_left),
        send(left.at[:, 0, 0], tok.at[:, 7, 3], lefty),
    ]

    krow, kcol = token_place(lax.broadcasted_iota(i32, (64, 128), 0))
    qrow, qcol = token_place(lax.broadcasted_iota(i32, (64, 128), 1) % 64)
    offset = (qrow - krow + 7) * 16 + qcol - kcol + 7
    low, low_half = offset % 128, offset < 128
    first_head = lax.broadcasted_iota(i32, (64, 128), 1) < 64

    def bias_of(head):
        at = functools.partial(jnp.take_along_axis, indices=low, axis=1, mode="promise_in_bounds")
        one_half = at(jnp.broadcast_to(table_ref[head:head + 1, 0:128], (64, 128)))
        return jnp.where(low_half, one_half, at(jnp.broadcast_to(table_ref[head:head + 1, 128:256], (64, 128))))

    for duo in range(4):
        bias_ref[duo // 2, :, (duo % 2) * 128:(duo % 2) * 128 + 128] = jnp.where(
            first_head, bias_of(2 * duo), bias_of(2 * duo + 1))

    def chunk(step):
        return slice(step * 128, step * 128 + 128)

    def project(step):
        part = chunk(step)
        value = tok[0, 2 * step:2 * step + 2].reshape(128, 1024).astype(f32)
        inverse = lax.rsqrt(jnp.mean(value * value, axis=1, keepdims=True) + EPS)
        inv_ref[part, :] = inverse
        normed = (value * inverse * gain_ref[...]).astype(bf16)
        upstream = tok[1, 2 * step:2 * step + 2].reshape(128, 1024)
        norm_t[step] = normed.T
        g_t[step] = upstream.T
        proj[part, :] = nn(normed, wqkv_ref[...]).astype(bf16)
        gheads[part, :] = nt(upstream, wout_ref[...]).astype(bf16)

    head_row = lax.broadcasted_iota(i32, (GROUP, GROUP), 0) // HEAD
    head_lane = lax.broadcasted_iota(i32, (GROUP, GROUP), 1) // HEAD
    diagonal = head_row == head_lane
    lane64 = lax.broadcasted_iota(i32, (64, GROUP), 1) // HEAD

    def spread(value):
        return jnp.where(diagonal, jnp.concatenate([value] * 4, axis=0), jnp.zeros((), value.dtype))

    def gather_heads(full):
        out = full[0:64]
        for h in range(1, 4):
            out = jnp.where(lane64 == h, full[h * 64:h * 64 + 64], out)
        return out

    def attend(win, grp):
        part = pl.ds(pl.multiple_of(win * 64, 64), 64)
        lo = grp * GROUP
        cq = slice(lo, lo + GROUP)
        ck = slice(all_heads + lo, all_heads + lo + GROUP)
        cv = slice(2 * all_heads + lo, 2 * all_heads + lo + GROUP)
        q, k, v, go = proj[part, cq], proj[part, ck], proj[part, cv], gheads[part, cq]
        q_wide, go_wide = spread(q), spread(go)
        scores = nt(k, q_wide) * scale + bias_ref[grp]
        expo = jnp.exp(scores - jnp.max(scores, axis=0, keepdims=True))
        soft = expo * (1.0 / jnp.sum(expo, axis=0, keepdims=True))
        soft_b = soft.astype(bf16)
        gp = nt(v, go_wide)
        inner = jnp.sum(gp * soft, axis=0, keepdims=True)
        gs = (soft * (gp - inner) * scale).astype(bf16)
        heads[part, cq] = gather_heads(tn(soft_b, v)).astype(bf16)
        gproj[part, cq] = gather_heads(tn(gs, k)).astype(bf16)
        gproj[part, ck] = nn(gs, q_wide).astype(bf16)
        gproj[part, cv] = nn(soft_b, go_wide).astype(bf16)

    def attend_range(first, last, grp):
        def body(win, carry):
            attend(win, grp)
            return carry

        lax.fori_loop(first, last, body, 0)

    def weights(grp, half):
        lo = grp * GROUP

        def body(step, carry):
            rows = pl.ds(pl.multiple_of(half * 512 + step * 128, 128), 128)
            from_norm = jnp.concatenate([norm_t[t, rows, :] for t in range(4)], axis=1)
            from_g = jnp.concatenate([g_t[t, rows, :] for t in range(4)], axis=1)
            zs = pl.ds(step * 2, 2)
            for kind in range(3):
                cols = slice(kind * all_heads + lo, kind * all_heads + lo + GROUP)
                value = nn(from_norm, gproj[:, cols]).astype(bf16)
                m_ref[grp, half, zs, :, :, :, kind * GROUP:kind * GROUP + GROUP] = value.reshape(2, 2, 2, 16, GROUP)
            value = nn(from_g, heads[:, lo:lo + GROUP]).astype(bf16)
            m_ref[grp, half, zs, :, :, :, 3 * GROUP:] = value.reshape(2, 2, 2, 16, GROUP)
            return carry

        lax.fori_loop(0, nz // 2, body, 0)
        return send(m_ref.at[grp, half, :, :, 1 - core], recv0.at[grp, half], pair)

    def exchange(source, target, axis):
        return [send(source.at[on(axis, s)[0]], target.at[s - 1], on(axis, s)[1]) for s in range(1, size[axis])]

    def pair_add(index):
        order, grp, lo = PARTS[index]
        wide = 512 // nx

        def body(block, carry):
            a, b, c = block // (2 * nz), (block // 2) % nz, block % 2
            for part in range(nx):
                cols = slice(lo + part * wide, lo + part * wide + wide)
                at = {"x": part, "y": a * 2 + c, "z": b}
                acc1[index][at[order[0]], at[order[1]], at[order[2]]] = (
                    m_ref[grp, a, b, c, core, :, cols] + recv0[grp, a, b, c, :, cols])
            return carry

        lax.fori_loop(0, 4 * nz, body, 0)
        return exchange(acc1[index], rx1[index], order[0])

    def sum_one(index, arrivals):
        order = PARTS[index][0]
        landed(arrivals)
        mine = place[order[0]]

        def body(j, carry):
            for k in range(size[order[2]]):
                value = acc1[index][mine, j, k].astype(f32)
                for s in range(size[order[0]] - 1):
                    value = value + rx1[index][s, j, k].astype(f32)
                acc2[index][j, k] = value.astype(bf16)
            return carry

        lax.fori_loop(0, size[order[1]], body, 0)
        return exchange(acc2[index], rx2[index], order[1])

    def sum_two(index, arrivals):
        order = PARTS[index][0]
        landed(arrivals)
        mine = place[order[1]]
        for k in range(size[order[2]]):
            value = acc2[index][mine, k].astype(f32)
            for s in range(size[order[1]] - 1):
                value = value + rx2[index][s, k].astype(f32)
            acc3[index][k] = value.astype(bf16)
        return exchange(acc3[index], rx3[index], order[2])

    def sum_three(index, arrivals):
        order = PARTS[index][0]
        landed(arrivals)
        value = acc3[index][place[order[2]]].astype(f32)
        for s in range(size[order[2]] - 1):
            value = value + rx3[index][s].astype(f32)
        return value

    def finish(step):
        part = chunk(step)
        att = nn(heads[part, :], wout_ref[...]).astype(bf16)
        grad_normed = nt(gproj[part, :], wqkv_ref[...])
        inverse = inv_ref[part, :]
        unit = tok[0, 2 * step:2 * step + 2].reshape(128, 1024).astype(f32) * inverse
        grad_unit = grad_normed * gain_ref[...]
        mean = jnp.mean(grad_unit * unit, axis=1, keepdims=True)
        ret[0, 2 * step:2 * step + 2] = att.reshape(2, 4, 16, 1024)
        ret[1, 2 * step:2 * step + 2] = (inverse * (grad_unit - unit * mean)).astype(bf16).reshape(2, 4, 16, 1024)

    def residual(rb):
        for which, ref, target in ((0, img_ref, out_ref), (1, cot_ref, gimg_ref)):
            value = jnp.concatenate(
                [block_at(ret, back, which, block_place(rb, cb))[...] for cb in range(8)], axis=0)
            value = nn(from_block, value).reshape(4, 32, 1024)
            target[rb * 4:rb * 4 + 4] = (ref[rb * 4:rb * 4 + 4].astype(f32) + value).astype(bf16)

    for copy in copies:
        copy.wait()
    project(0)
    attend_range(0, 2, 0)
    landed(from_right)
    project(1)
    attend_range(2, 4, 0)
    landed(from_below)
    project(2)
    attend_range(4, 6, 0)
    landed(from_above)
    project(3)
    attend_range(6, 8, 0)
    paired0 = [weights(0, 0), weights(0, 1)]
    attend_range(0, 4, 1)
    landed(paired0)
    p0 = pair_add(0)
    p1 = pair_add(1)
    attend_range(4, 8, 1)
    paired1 = [weights(1, 0), weights(1, 1)]
    finish(2)
    b_above = [send(ret.at[:, 4:6, 2:4], b_up, below)]
    p1 = sum_one(1, p1)
    landed(paired1)
    p2 = pair_add(2)
    p3 = pair_add(3)
    finish(3)
    b_below = [
        send(ret.at[:, 6, 0], b_down.at[:, 0, 0], above),
        send(ret.at[:, 6, 1], b_down.at[:, 1, 0], above),
        send(ret.at[:, 7, 0], b_down.at[:, 2, 0], above),
    ]
    b_lefty = [
        send(ret.at[:, 7, 1], b_corner.at[:, 0, 0], above_right),
        send(ret.at[:, 7, 3], b_left.at[:, 0, 0], right),
    ]
    p0 = sum_one(0, p0)
    finish(1)
    b_lefty += [
        send(ret.at[:, 3, 1], b_left.at[:, 1, 0], right),
        send(ret.at[:, 3, 3], b_left.at[:, 2, 0], right),
    ]
    p1 = sum_two(1, p1)
    finish(0)
    p0 = sum_two(0, p0)
    p2 = sum_one(2, p2)
    p3 = sum_one(3, p3)
    landed(b_lefty)
    residual(1)
    residual(2)
    p2 = sum_two(2, p2)
    p3 = sum_two(3, p3)
    landed(b_above)
    residual(0)
    landed(b_below)
    residual(3)
    sums = [sum_three(0, p0), sum_three(1, p1), sum_three(2, p2), sum_three(3, p3)]
    near, far = jnp.concatenate(sums[0:2], axis=1), jnp.concatenate(sums[2:4], axis=1)
    for other in range(nx):
        swap_out[other, 0:4] = near[other * 4:other * 4 + 4]
        swap_out[other, 4:8] = far[other * 4:other * 4 + 4]
    last = exchange(swap_out, swap_in, "x")
    swap_in[nx - 1] = swap_out[x]
    landed(last)
    wide = 512 // nx
    for source in range(nx):
        got = swap_in[(x - source + nx - 1) % nx] * factor
        for index in range(count_parts):
            grp, lo = PARTS[index][1:]
            value = got[(index // 2) * 4:(index // 2) * 4 + 4, (index % 2) * wide:(index % 2) * wide + wide]
            kind, within = divmod(lo + source * wide, GROUP)
            if kind < 3:
                start = kind * all_heads + grp * GROUP + within
                gqkv_ref[:, start:start + wide] = value
            else:
                start = grp * GROUP + within
                gout_ref[:, start:start + wide] = value
    block = yh * (4 * nz) + z * 4 + yl * 2 + core
    own_rows = wqkv_ref[pl.ds(pl.multiple_of(block * 16, 16), 16), :].astype(f32)
    own = own_rows[0:4]
    for other in range(1, nx):
        own = jnp.where(x == other, own_rows[other * 4:other * 4 + 4], own)
    ggain_ref[...] = jnp.broadcast_to(jnp.sum(own * gqkv_ref[...], axis=1, keepdims=True), (4, 128))
    for copy in started:
        copy.wait_send()


def block(image, cotangent, gain, w_qkv, w_out, bias_table, nz, nx, factor):
    f32, bf16 = jnp.float32, jnp.bfloat16
    features = image.shape[-1]
    table = jnp.pad(bias_table, ((0, 0), (0, 1), (0, 1))).reshape(8, 256)
    size = {"x": nx, "y": 4, "z": nz}
    wide = 512 // nx
    orders = [part[0] for part in PARTS]
    dims = [[size[axis] for axis in order] for order in orders]
    shapes = [
        (w_qkv.shape, bf16), (w_out.shape, bf16),
        ((2, 8, 4, 16, features), bf16), ((2, 8, 4, 16, features), bf16),
    ]
    for _ in range(2):
        shapes += [((2, 2, 2, 16, features), bf16), ((2, 3, 1, 16, features), bf16),
                   ((2, 3, 1, 16, features), bf16), ((2, 1, 1, 16, features), bf16)]
    shapes += [
        ((4, features, 128), bf16), ((4, features, 128), bf16), ((512, 1), f32),
        ((512, 1536), bf16), ((512, 512), bf16), ((512, 512), bf16), ((512, 1536), bf16), ((2, 64, 256), f32),
        ((2, 2, nz, 2, 2, 16, 1024), bf16), ((2, 2, nz, 2, 16, 1024), bf16),
    ]
    shapes += [((a, b, c, 16, wide), bf16) for a, b, c in dims]
    shapes += [((b, c, 16, wide), bf16) for a, b, c in dims]
    shapes += [((c, 16, wide), bf16) for a, b, c in dims]
    shapes += [((a - 1, b, c, 16, wide), bf16) for a, b, c in dims]
    shapes += [((b - 1, c, 16, wide), bf16) for a, b, c in dims]
    shapes += [((c - 1, 16, wide), bf16) for a, b, c in dims]
    shapes += [((nx, 8, 2 * wide), f32), ((nx, 8, 2 * wide), f32)]
    count = 8 + 4 + 8 + len(PARTS) * (nx + nz + 4 - 3) + nx - 1
    vmem, hbm = pl.BlockSpec(memory_space=pltpu.VMEM), pl.BlockSpec(memory_space=pl.ANY)
    return pl.pallas_call(
        functools.partial(kernel, nz, nx, factor),
        out_shape=(
            jax.ShapeDtypeStruct(image.shape, bf16), jax.ShapeDtypeStruct(image.shape, bf16),
            jax.ShapeDtypeStruct((4, 1536), f32), jax.ShapeDtypeStruct((4, 512), f32),
            jax.ShapeDtypeStruct((4, 128), f32),
        ),
        in_specs=[vmem, vmem, vmem, hbm, hbm, vmem],
        out_specs=(vmem,) * 5,
        scratch_shapes=[pltpu.VMEM(shape, kind) for shape, kind in shapes]
        + [pltpu.SemaphoreType.DMA((count,)), pltpu.SemaphoreType.DMA((count,)), pltpu.SemaphoreType.DMA((2,))],
        compiler_params=pltpu.CompilerParams(
            collective_id=0, has_side_effects=True, vmem_limit_bytes=56 * 1024 * 1024),
        name="window_block",
    )(image, cotangent, gain.reshape(1, features), w_qkv, w_out, table)


def local(image, cotangent, gain, w_qkv, w_out, bias_table):
    total_count = (
        lax.axis_size("rows")
        * lax.axis_size("cols")
        * lax.axis_size("rep")
        * image.shape[1]
        * image.shape[2]
    )
    factor = 1.0 / float(np.sqrt(total_count))
    result, grad_result, grad_qkv, grad_out, gain_sum = block(
        image[0], cotangent[0], gain, w_qkv, w_out, bias_table,
        lax.axis_size("rows") // 2, lax.axis_size("rep"), factor)
    first = 4 * ((lax.axis_index("rows") * 4 + lax.axis_index("cols")) * 4 + lax.axis_index("rep"))
    own_gain = lax.dynamic_slice_in_dim(gain, first, 4, 0)
    return (result[None], grad_result[None], grad_qkv, grad_out.T, gain_sum[:, 0] / own_gain)


def solution(mesh):
    in_specs = (P("rep", "rows", "cols", None), P("rep", "rows", "cols", None), P(), P(), P(), P())
    out_specs = (
        P("rep", "rows", "cols", None),
        P("rep", "rows", "cols", None),
        P(("rows", "cols", "rep"), None),
        P(None, ("rows", "cols", "rep")),
        P(("rows", "cols", "rep")),
    )
    return jax.shard_map(local, mesh=mesh, in_specs=in_specs, out_specs=out_specs, check_vma=False)
```

time: 453 us -> 82.4 us (0.18)
  waiting for transfers between devices: 200 us -> 0 us
  local copies, waits for them, and re-layouts: 90 us -> 8.12 us
  blocking collectives: 75.5 us -> 0 us
  Pallas kernels: 0 us -> 70.7 us
  matrix products: 37.6 us -> 0 us
  other arithmetic: 22.7 us -> 1.28 us
  between operations: 14.3 us -> 0.68 us
  starting transfers between devices: 11.8 us -> 0 us
    unnamed x2 -> x0, waiting for transfers between devices: 167 us -> none
    unnamed x1 -> x0, blocking collectives: 75.5 us -> none
    pallas_call x0 -> x1, Pallas kernels: none -> 70.7 us  [block(): pl.pallas_call(functools.partial(kernel, nz, nx, factor), out_shape=(jax....]
    gather x2 -> x0, local copies, waits for them, and re-layouts: 48 us -> none  [window_block(): bias = bias_table[:, row_offset, col_offset]]
    dot_general x11 -> x0, matrix products: 33.6 us -> none  [the longest x4 11.1 us: contract(): lax.dot_general(left, right, (((left_dim,), (right_dim,)), ((), ())), pre...]
    ppermute x4 -> x0, waiting for transfers between devices: 32.4 us -> none  [passed_along(): return lax.ppermute(value, axis, pairs)]
    another operation x9 -> x0, local copies, waits for them, and re-layouts: 24.9 us -> none  [the longest x2 7.9 us: from_windows(): blocks.reshape(rows_n // window, cols_n // window, window, window, chans)]
    ppermute x4 -> x0, starting transfers between devices: 11.8 us -> none  [passed_along(): return lax.ppermute(value, axis, pairs)]
  transfers between devices with their start and end apart: 5 -> 0, of which waited for: 3 -> 0; matrix products, arithmetic and copies ran while one was open for 14% -> 0% of each run, Pallas kernels for 0% -> 0%
where the time goes in v3:
time: 82.4 us; the launch traced here: 80.7 us
  Pallas kernels  70.7 us (86%)
  local copies, waits for them, and re-layouts  8.12 us (10%)
  other arithmetic  1.28 us (2%)
    pallas_call x1, Pallas kernels, block(): pl.pallas_call(functools.partial(kernel, nz, nx, factor), out_shape=(jax....  70.7 us
    unnamed x9, local copies, waits for them, and re-layouts  6.63 us

profile of v3, /device:TPU:1, one launch (start us, length us, event | category | flops | bytes accessed | tf_op | source)
XLA Modules:
  0.0 80.7 jit_solution(4153716201810854571)
XLA Ops:
  0.6 0.8 %copy.13 = f32[8,15,15]{2,1,0:T(8,128)S(1)} copy(f32[8,15,15]{2,0,1:T(8,128)} %param.11) | data formatting | bytes 14400
  1.5 0.7 reshape.17.table_ref
  2.2 70.7 %window_block.1 = (bf16[16,32,1024]{2,1,0:T(8,128)(2,1)}, bf16[16,32,1024]{2,1,0:T(8,128)(2,1)}, f32[4,1536]{1,0:T(4,128)}, f32[4,512]{1,0:T(4,128)}, f32[4,128]{1,0:T(4,128)}) custom-call(bf16[16,32,1024]{2,1,0:T(8,128)(2,1)} %bitcast.8, bf16[16,32,1024]{2,1,0:T(8,128)(2,1)} %bitcast.9, f32[1,1024]{1,0:T(1,128)} %bitcast.11, bf16[1024,1536]{1,0:T(8,128)(2,1)} %wqkv_hbm.1, ...), custom_call_target="tpu_custom_call" | custom-call | tf_op jit(solution)/shard_map/window_block/pallas_call | solution.py:424
  72.9 0.0 copy-start
  72.9 0.0 copy-start.1
  72.9 0.8 slice_reduce_fusion
  73.7 1.3 %dynamic-slice_divide_fusion = f32[4]{0:T(128)} fusion(f32[4]{0:T(128)S(1)} %slice_reduce_fusion, f32[1024]{0:T(1024)} %param.8, s32[]{:T(128)S(6)} %select_n.3), kind=kLoop, calls=%fused_computation.1 | loop fusion | flops 4 | bytes 52 | tf_op jit(solution)/shard_map/div | solution.py:455
  75.0 2.3 %copy.18 = bf16[1,16,32,1024]{3,2,1,0:T(8,128)(2,1)} copy(bf16[1,16,32,1024]{3,2,1,0:T(8,128)(2,1)} %bitcast.7) | data formatting | bytes 2097152
  77.2 2.3 %copy.19 = bf16[1,16,32,1024]{3,2,1,0:T(8,128)(2,1)} copy(bf16[1,16,32,1024]{3,2,1,0:T(8,128)(2,1)} %bitcast.6) | data formatting | bytes 2097152
  79.5 0.0 copy-done
  79.5 0.6 copy.20
  80.1 0.0 copy-done.1
  80.1 0.6 copy.21
  (1 shorter events, 0.0 us)
Async XLA Ops:
  72.9 6.7 %copy-start = (f32[4,1536]{1,0:T(4,128)S(1)}, f32[4,1536]{1,0:T(4,128)}, u32[]{:S(2)}) copy-start(f32[4,1536]{1,0:T(4,128)} %get-tuple-element.22) | copy-start | bytes 73732
  72.9 7.3 %copy-start.1 = (f32[4,512]{1,0:T(4,128)S(1)}, f32[4,512]{1,0:T(4,128)}, u32[]{:S(2)}) copy-start(f32[4,512]{1,0:T(4,128)} %get-tuple-element.13) | copy-start | bytes 24580

commit v4 on v3

--- a/solution.py
+++ b/solution.py
@@ -12,7 +12,7 @@
 EPS = 1e-06
 GROUP = 256
 HEAD = 64
-PARTS = (("zxy", 0, 0), ("xyz", 0, 512), ("yzx", 1, 0), ("xyz", 1, 512))
+PARTS = (("yxz", 0, 0), ("xyz", 0, 512), ("yxz", 1, 0), ("xyz", 1, 512))
 
 
 def token_place(index):
@@ -44,17 +44,17 @@
 
 
 def kernel(nz, nx, factor,
-           img_ref, cot_ref, gain_ref, wqkv_hbm, wout_hbm, table_ref,
-           out_ref, gimg_ref, gqkv_ref, gout_ref, ggain_ref,
+           img_ref, cot_ref, gain_ref, wqkv_hbm, wout_hbm, table3_ref,
+           att_ref, gtok_ref, gqkv_ref, gout_ref, ggain_ref,
            wqkv_ref, wout_ref, tok, ret,
            up, down, left, corner, b_up, b_down, b_left, b_corner,
-           norm_t, g_t, inv_ref, proj, gheads, heads, gproj, bias_ref,
+           norm_t, g_t, inv_ref, proj, gheads, heads, gproj, bias_ref, table_ref,
            m_ref, recv0, *rest):
     f32, bf16, i32 = jnp.float32, jnp.bfloat16, jnp.int32
     count_parts = len(PARTS)
     acc1, acc2, acc3 = rest[0:4], rest[4:8], rest[8:12]
     rx1, rx2, rx3 = rest[12:16], rest[16:20], rest[20:24]
-    swap_out, swap_in, sends, recvs, local_sems = rest[24:]
+    sends, recvs, local_sems = rest[24:]
     scale = HEAD ** -0.5
     all_heads = 2 * GROUP
 
@@ -148,6 +148,9 @@
     offset = (qrow - krow + 7) * 16 + qcol - kcol + 7
     low, low_half = offset % 128, offset < 128
     first_head = lax.broadcasted_iota(i32, (64, 128), 1) < 64
+
+    for dr in range(15):
+        table_ref[:, dr * 16:dr * 16 + 15] = table3_ref[dr]
 
     def bias_of(head):
         at = functools.partial(jnp.take_along_axis, indices=low, axis=1, mode="promise_in_bounds")
@@ -238,15 +241,16 @@
 
     def pair_add(index):
         order, grp, lo = PARTS[index]
-        wide = 512 // nx
 
         def body(block, carry):
             a, b, c = block // (2 * nz), (block // 2) % nz, block % 2
+            cols = slice(lo, lo + 512)
+            value = m_ref[grp, a, b, c, core, :, cols].astype(f32) + recv0[grp, a, b, c, :, cols].astype(f32)
             for part in range(nx):
-                cols = slice(lo + part * wide, lo + part * wide + wide)
+                rows = value[part * 4:part * 4 + 4]
+                tile = jnp.concatenate([rows[:, j * 128:j * 128 + 128] for j in range(4)], axis=0)
                 at = {"x": part, "y": a * 2 + c, "z": b}
-                acc1[index][at[order[0]], at[order[1]], at[order[2]]] = (
-                    m_ref[grp, a, b, c, core, :, cols] + recv0[grp, a, b, c, :, cols])
+                acc1[index][at[order[0]], at[order[1]], at[order[2]]] = tile.astype(bf16)
             return carry
 
         lax.fori_loop(0, 4 * nz, body, 0)
@@ -299,11 +303,10 @@
         ret[1, 2 * step:2 * step + 2] = (inverse * (grad_unit - unit * mean)).astype(bf16).reshape(2, 4, 16, 1024)
 
     def residual(rb):
-        for which, ref, target in ((0, img_ref, out_ref), (1, cot_ref, gimg_ref)):
+        for which, target in ((0, att_ref), (1, gtok_ref)):
             value = jnp.concatenate(
                 [block_at(ret, back, which, block_place(rb, cb))[...] for cb in range(8)], axis=0)
-            value = nn(from_block, value).reshape(4, 32, 1024)
-            target[rb * 4:rb * 4 + 4] = (ref[rb * 4:rb * 4 + 4].astype(f32) + value).astype(bf16)
+            target[rb * 4:rb * 4 + 4] = nn(from_block, value).astype(bf16).reshape(4, 32, 1024)
 
     for copy in copies:
         copy.wait()
@@ -312,6 +315,7 @@
     landed(from_right)
     project(1)
     attend_range(2, 4, 0)
+    attend_range(0, 4, 1)
     landed(from_below)
     project(2)
     attend_range(4, 6, 0)
@@ -319,15 +323,14 @@
     project(3)
     attend_range(6, 8, 0)
     paired0 = [weights(0, 0), weights(0, 1)]
-    attend_range(0, 4, 1)
+    attend_range(4, 6, 1)
     landed(paired0)
     p0 = pair_add(0)
     p1 = pair_add(1)
-    attend_range(4, 8, 1)
+    attend_range(6, 8, 1)
     paired1 = [weights(1, 0), weights(1, 1)]
     finish(2)
     b_above = [send(ret.at[:, 4:6, 2:4], b_up, below)]
-    p1 = sum_one(1, p1)
     landed(paired1)
     p2 = pair_add(2)
     p3 = pair_add(3)
@@ -342,14 +345,15 @@
         send(ret.at[:, 7, 3], b_left.at[:, 0, 0], right),
     ]
     p0 = sum_one(0, p0)
+    p1 = sum_one(1, p1)
     finish(1)
     b_lefty += [
         send(ret.at[:, 3, 1], b_left.at[:, 1, 0], right),
         send(ret.at[:, 3, 3], b_left.at[:, 2, 0], right),
     ]
-    p1 = sum_two(1, p1)
     finish(0)
     p0 = sum_two(0, p0)
+    p1 = sum_two(1, p1)
     p2 = sum_one(2, p2)
     p3 = sum_one(3, p3)
     landed(b_lefty)
@@ -361,33 +365,29 @@
     residual(0)
     landed(b_below)
     residual(3)
-    sums = [sum_three(0, p0), sum_three(1, p1), sum_three(2, p2), sum_three(3, p3)]
-    near, far = jnp.concatenate(sums[0:2], axis=1), jnp.concatenate(sums[2:4], axis=1)
-    for other in range(nx):
-        swap_out[other, 0:4] = near[other * 4:other * 4 + 4]
-        swap_out[other, 4:8] = far[other * 4:other * 4 + 4]
-    last = exchange(swap_out, swap_in, "x")
-    swap_in[nx - 1] = swap_out[x]
-    landed(last)
-    wide = 512 // nx
-    for source in range(nx):
-        got = swap_in[(x - source + nx - 1) % nx] * factor
-        for index in range(count_parts):
-            grp, lo = PARTS[index][1:]
-            value = got[(index // 2) * 4:(index // 2) * 4 + 4, (index % 2) * wide:(index % 2) * wide + wide]
-            kind, within = divmod(lo + source * wide, GROUP)
+    arrivals = [p0, p1, p2, p3]
+    for index in range(count_parts):
+        grp, lo = PARTS[index][1:]
+        got = sum_three(index, arrivals[index]) * factor
+        for j in range(4):
+            kind, within = divmod(lo + j * 128, GROUP)
+            start = grp * GROUP + within
             if kind < 3:
-                start = kind * all_heads + grp * GROUP + within
-                gqkv_ref[:, start:start + wide] = value
+                start += kind * all_heads
+                gqkv_ref[:, start:start + 128] = got[j * 4:j * 4 + 4]
             else:
-                start = grp * GROUP + within
-                gout_ref[:, start:start + wide] = value
+                gout_ref[:, start:start + 128] = got[j * 4:j * 4 + 4]
     block = yh * (4 * nz) + z * 4 + yl * 2 + core
     own_rows = wqkv_ref[pl.ds(pl.multiple_of(block * 16, 16), 16), :].astype(f32)
     own = own_rows[0:4]
     for other in range(1, nx):
         own = jnp.where(x == other, own_rows[other * 4:other * 4 + 4], own)
-    ggain_ref[...] = jnp.broadcast_to(jnp.sum(own * gqkv_ref[...], axis=1, keepdims=True), (4, 128))
+    lane = lax.broadcasted_iota(i32, (4, 1024), 1)
+    mine = lane == (block * nx + x) * 4 + lax.broadcasted_iota(i32, (4, 1024), 0)
+    own_gain = jnp.sum(jnp.where(mine, gain_ref[...], 0.0), axis=1, keepdims=True)
+    value = jnp.sum(own * gqkv_ref[...], axis=1, keepdims=True) / own_gain
+    spot = lax.broadcasted_iota(i32, (4, 128), 0) == lax.broadcasted_iota(i32, (4, 128), 1)
+    ggain_ref[...] = jnp.sum(jnp.where(spot, value, 0.0), axis=0, keepdims=True)[:, 0:4]
     for copy in started:
         copy.wait_send()
 
@@ -395,9 +395,9 @@
 def block(image, cotangent, gain, w_qkv, w_out, bias_table, nz, nx, factor):
     f32, bf16 = jnp.float32, jnp.bfloat16
     features = image.shape[-1]
-    table = jnp.pad(bias_table, ((0, 0), (0, 1), (0, 1))).reshape(8, 256)
+    table = bias_table.transpose(1, 0, 2)
     size = {"x": nx, "y": 4, "z": nz}
-    wide = 512 // nx
+    wide = 128
     orders = [part[0] for part in PARTS]
     dims = [[size[axis] for axis in order] for order in orders]
     shapes = [
@@ -409,7 +409,7 @@
                    ((2, 3, 1, 16, features), bf16), ((2, 1, 1, 16, features), bf16)]
     shapes += [
         ((4, features, 128), bf16), ((4, features, 128), bf16), ((512, 1), f32),
-        ((512, 1536), bf16), ((512, 512), bf16), ((512, 512), bf16), ((512, 1536), bf16), ((2, 64, 256), f32),
+        ((512, 1536), bf16), ((512, 512), bf16), ((512, 512), bf16), ((512, 1536), bf16), ((2, 64, 256), f32), ((8, 256), f32),
         ((2, 2, nz, 2, 2, 16, 1024), bf16), ((2, 2, nz, 2, 16, 1024), bf16),
     ]
     shapes += [((a, b, c, 16, wide), bf16) for a, b, c in dims]
@@ -418,15 +418,14 @@
     shapes += [((a - 1, b, c, 16, wide), bf16) for a, b, c in dims]
     shapes += [((b - 1, c, 16, wide), bf16) for a, b, c in dims]
     shapes += [((c - 1, 16, wide), bf16) for a, b, c in dims]
-    shapes += [((nx, 8, 2 * wide), f32), ((nx, 8, 2 * wide), f32)]
-    count = 8 + 4 + 8 + len(PARTS) * (nx + nz + 4 - 3) + nx - 1
+    count = 8 + 4 + 8 + len(PARTS) * (nx + nz + 4 - 3)
     vmem, hbm = pl.BlockSpec(memory_space=pltpu.VMEM), pl.BlockSpec(memory_space=pl.ANY)
     return pl.pallas_call(
         functools.partial(kernel, nz, nx, factor),
         out_shape=(
             jax.ShapeDtypeStruct(image.shape, bf16), jax.ShapeDtypeStruct(image.shape, bf16),
             jax.ShapeDtypeStruct((4, 1536), f32), jax.ShapeDtypeStruct((4, 512), f32),
-            jax.ShapeDtypeStruct((4, 128), f32),
+            jax.ShapeDtypeStruct((1, 4), f32),
         ),
         in_specs=[vmem, vmem, vmem, hbm, hbm, vmem],
         out_specs=(vmem,) * 5,
@@ -438,6 +437,35 @@
     )(image, cotangent, gain.reshape(1, features), w_qkv, w_out, table)
 
 
+def add_kernel(img_ref, cot_ref, att_ref, gtok_ref, gqkv_in, gout_in, ggain_in,
+               out_ref, gimg_ref, gqkv_ref, gout_ref, ggain_ref):
+    f32, bf16 = jnp.float32, jnp.bfloat16
+    out_ref[...] = (img_ref[...].astype(f32) + att_ref[...].astype(f32)).astype(bf16)
+    gimg_ref[...] = (cot_ref[...].astype(f32) + gtok_ref[...].astype(f32)).astype(bf16)
+    gqkv_ref[...] = gqkv_in[...]
+    gout_ref[...] = gout_in[...]
+    ggain_ref[...] = ggain_in[...]
+
+
+def add_branches(image, cotangent, attention, grad_tokens, grad_qkv, grad_out, grad_gain):
+    rows, cols, features = image.shape
+    steps = 4
+    tile = pl.BlockSpec((rows // steps, cols, features), lambda i: (i, 0, 0))
+    small = [pl.BlockSpec(value.shape, lambda i: (0, 0)) for value in (grad_qkv, grad_out, grad_gain)]
+    return pl.pallas_call(
+        add_kernel,
+        grid=(steps,),
+        out_shape=(
+            jax.ShapeDtypeStruct(image.shape, image.dtype), jax.ShapeDtypeStruct(image.shape, image.dtype),
+            jax.ShapeDtypeStruct(grad_qkv.shape, jnp.float32), jax.ShapeDtypeStruct(grad_out.shape, jnp.float32),
+            jax.ShapeDtypeStruct(grad_gain.shape, jnp.float32),
+        ),
+        in_specs=[tile] * 4 + small,
+        out_specs=(tile, tile, *small),
+        name="add_branches",
+    )(image, cotangent, attention, grad_tokens, grad_qkv, grad_out, grad_gain)
+
+
 def local(image, cotangent, gain, w_qkv, w_out, bias_table):
     total_count = (
         lax.axis_size("rows")
@@ -447,12 +475,11 @@
         * image.shape[2]
     )
     factor = 1.0 / float(np.sqrt(total_count))
-    result, grad_result, grad_qkv, grad_out, gain_sum = block(
+    branches = block(
         image[0], cotangent[0], gain, w_qkv, w_out, bias_table,
         lax.axis_size("rows") // 2, lax.axis_size("rep"), factor)
-    first = 4 * ((lax.axis_index("rows") * 4 + lax.axis_index("cols")) * 4 + lax.axis_index("rep"))
-    own_gain = lax.dynamic_slice_in_dim(gain, first, 4, 0)
-    return (result[None], grad_result[None], grad_qkv, grad_out.T, gain_sum[:, 0] / own_gain)
+    result, grad_result, grad_qkv, grad_out, grad_gain = add_branches(image[0], cotangent[0], *branches)
+    return (result[None], grad_result[None], grad_qkv, grad_out.T, grad_gain.reshape(4))
 
 
 def solution(mesh):

time: 82.4 us -> 71.8 us (0.87); the launches traced: 80.7 us -> 71.6 us
  local copies, waits for them, and re-layouts: 8.12 us -> 0 us
  other arithmetic: 1.28 us -> 0 us
    unnamed x9 -> x0, local copies, waits for them, and re-layouts: 6.63 us -> none
    pallas_call x0 -> x1, Pallas kernels: none -> 4.19 us  [add_branches(): pl.pallas_call(add_kernel, grid=(steps,), out_shape=(jax.ShapeDtypeStruct...]
    pallas_call x1, Pallas kernels: 70.7 us -> 66.8 us  [block(): pl.pallas_call(functools.partial(kernel, nz, nx, factor), out_shape=(jax....]
    div x1 -> x0, other arithmetic: 1.28 us -> none  [local(): gain_sum[:, 0] / own_gain]
where the time goes in v4:
time: 71.8 us; the launch traced here: 71.6 us
  Pallas kernels  71 us (99%)
    pallas_call x1, Pallas kernels, block(): pl.pallas_call(functools.partial(kernel, nz, nx, factor), out_shape=(jax....  66.8 us
    pallas_call x1, Pallas kernels, add_branches(): pl.pallas_call(add_kernel, grid=(steps,), out_shape=(jax.ShapeDtypeStruct...  4.19 us

profile of v4, /device:TPU:1, one launch (start us, length us, event | category | flops | bytes accessed | tf_op | source)
XLA Modules:
  0.0 71.6 jit_solution(7710235604301312755)
XLA Ops:
  0.6 66.8 %window_block.1 = (bf16[16,32,1024]{2,1,0:T(8,128)(2,1)}, bf16[16,32,1024]{2,1,0:T(8,128)(2,1)}, f32[4,1536]{1,0:T(4,128)}, f32[4,512]{1,0:T(4,128)}, f32[1,4]{1,0:T(1,128)}) custom-call(bf16[16,32,1024]{2,1,0:T(8,128)(2,1)} %bitcast.8, bf16[16,32,1024]{2,1,0:T(8,128)(2,1)} %bitcast.10, f32[1,1024]{1,0:T(1,128)} %bitcast.13, bf16[1024,1536]{1,0:T(8,128)(2,1)} %wqkv_hbm.1, ...), custom_call_target="tpu_custom_call" | custom-call | tf_op jit(solution)/shard_map/window_block/pallas_call | solution.py:423
  67.4 4.2 %add_branches.1 = (bf16[16,32,1024]{2,1,0:T(8,128)(2,1)}, bf16[16,32,1024]{2,1,0:T(8,128)(2,1)}, f32[4,1536]{1,0:T(4,128)}, f32[4,512]{1,0:T(4,128)}, f32[1,4]{1,0:T(1,128)}) custom-call(bf16[16,32,1024]{2,1,0:T(8,128)(2,1)} %bitcast.9, bf16[16,32,1024]{2,1,0:T(8,128)(2,1)} %bitcast.11, bf16[16,32,1024]{2,1,0:T(8,128)(2,1)} %get-tuple-element.15.att_ref, ...), custom_call_target="tpu_custom_call" | custom-call | tf_op jit(solution)/shard_map/add_branches/pallas_call | solution.py:455

commit v5 on v4

--- a/solution.py
+++ b/solution.py
@@ -330,37 +330,37 @@
     attend_range(6, 8, 1)
     paired1 = [weights(1, 0), weights(1, 1)]
     finish(2)
-    b_above = [send(ret.at[:, 4:6, 2:4], b_up, below)]
     landed(paired1)
     p2 = pair_add(2)
     p3 = pair_add(3)
     finish(3)
-    b_below = [
-        send(ret.at[:, 6, 0], b_down.at[:, 0, 0], above),
-        send(ret.at[:, 6, 1], b_down.at[:, 1, 0], above),
-        send(ret.at[:, 7, 0], b_down.at[:, 2, 0], above),
-    ]
-    b_lefty = [
-        send(ret.at[:, 7, 1], b_corner.at[:, 0, 0], above_right),
-        send(ret.at[:, 7, 3], b_left.at[:, 0, 0], right),
-    ]
     p0 = sum_one(0, p0)
     p1 = sum_one(1, p1)
     finish(1)
-    b_lefty += [
-        send(ret.at[:, 3, 1], b_left.at[:, 1, 0], right),
-        send(ret.at[:, 3, 3], b_left.at[:, 2, 0], right),
-    ]
     finish(0)
     p0 = sum_two(0, p0)
     p1 = sum_two(1, p1)
     p2 = sum_one(2, p2)
     p3 = sum_one(3, p3)
+    b_above = [send(ret.at[:, 4:6, 2:4], b_up, below)]
+    b_below = [
+        send(ret.at[:, 6, 0], b_down.at[:, 0, 0], above),
+        send(ret.at[:, 6, 1], b_down.at[:, 1, 0], above),
+        send(ret.at[:, 7, 0], b_down.at[:, 2, 0], above),
+    ]
+    b_lefty = [
+        send(ret.at[:, 7, 1], b_corner.at[:, 0, 0], above_right),
+        send(ret.at[:, 7, 3], b_left.at[:, 0, 0], right),
+    ]
+    b_lefty += [
+        send(ret.at[:, 3, 1], b_left.at[:, 1, 0], right),
+        send(ret.at[:, 3, 3], b_left.at[:, 2, 0], right),
+    ]
+    p2 = sum_two(2, p2)
+    p3 = sum_two(3, p3)
     landed(b_lefty)
     residual(1)
     residual(2)
-    p2 = sum_two(2, p2)
-    p3 = sum_two(3, p3)
     landed(b_above)
     residual(0)
     landed(b_below)
@@ -449,7 +449,7 @@
 
 def add_branches(image, cotangent, attention, grad_tokens, grad_qkv, grad_out, grad_gain):
     rows, cols, features = image.shape
-    steps = 4
+    steps = 2
     tile = pl.BlockSpec((rows // steps, cols, features), lambda i: (i, 0, 0))
     small = [pl.BlockSpec(value.shape, lambda i: (0, 0)) for value in (grad_qkv, grad_out, grad_gain)]
     return pl.pallas_call(

time: 71.8 us -> 70.7 us (0.985)
  Pallas kernels: 71 us -> 69.9 us
    pallas_call x1, Pallas kernels: 4.19 us -> 3.37 us  [add_branches(): pl.pallas_call(add_kernel, grid=(steps,), out_shape=(jax.ShapeDtypeStruct...]
where the time goes in v5:
time: 70.7 us; the launch traced here: 70.6 us
  Pallas kernels  69.9 us (99%)
    pallas_call x1, Pallas kernels, block(): pl.pallas_call(functools.partial(kernel, nz, nx, factor), out_shape=(jax....  66.6 us
    pallas_call x1, Pallas kernels, add_branches(): pl.pallas_call(add_kernel, grid=(steps,), out_shape=(jax.ShapeDtypeStruct...  3.37 us

profile of v5, /device:TPU:1, one launch (start us, length us, event | category | flops | bytes accessed | tf_op | source)
XLA Modules:
  0.0 70.6 jit_solution(14330857394918351392)
XLA Ops:
  0.6 66.6 %window_block.1 = (bf16[16,32,1024]{2,1,0:T(8,128)(2,1)}, bf16[16,32,1024]{2,1,0:T(8,128)(2,1)}, f32[4,1536]{1,0:T(4,128)}, f32[4,512]{1,0:T(4,128)}, f32[1,4]{1,0:T(1,128)}) custom-call(bf16[16,32,1024]{2,1,0:T(8,128)(2,1)} %bitcast.8, bf16[16,32,1024]{2,1,0:T(8,128)(2,1)} %bitcast.10, f32[1,1024]{1,0:T(1,128)} %bitcast.13, bf16[1024,1536]{1,0:T(8,128)(2,1)} %wqkv_hbm.1, ...), custom_call_target="tpu_custom_call" | custom-call | tf_op jit(solution)/shard_map/window_block/pallas_call | solution.py:423
  67.2 3.4 %add_branches.1 = (bf16[16,32,1024]{2,1,0:T(8,128)(2,1)}, bf16[16,32,1024]{2,1,0:T(8,128)(2,1)}, f32[4,1536]{1,0:T(4,128)}, f32[4,512]{1,0:T(4,128)}, f32[1,4]{1,0:T(1,128)}) custom-call(bf16[16,32,1024]{2,1,0:T(8,128)(2,1)} %bitcast.9, bf16[16,32,1024]{2,1,0:T(8,128)(2,1)} %bitcast.11, bf16[16,32,1024]{2,1,0:T(8,128)(2,1)} %get-tuple-element.15.att_ref, ...), custom_call_target="tpu_custom_call" | custom-call | tf_op jit(solution)/shard_map/add_branches/pallas_call | solution.py:455

commit v6 on v5

--- a/solution.py
+++ b/solution.py
@@ -253,7 +253,7 @@
                 acc1[index][at[order[0]], at[order[1]], at[order[2]]] = tile.astype(bf16)
             return carry
 
-        lax.fori_loop(0, 4 * nz, body, 0)
+        lax.fori_loop(0, 4 * nz, body, 0, unroll=4)
         return exchange(acc1[index], rx1[index], order[0])
 
     def sum_one(index, arrivals):

time: 70.7 us -> 69.9 us (0.989)
  Pallas kernels: 69.9 us -> 69.1 us
    pallas_call x1, Pallas kernels: 66.6 us -> 65.8 us  [block(): pl.pallas_call(functools.partial(kernel, nz, nx, factor), out_shape=(jax....]
where the time goes in v6:
time: 69.9 us; the launch traced here: 69.8 us
  Pallas kernels  69.1 us (99%)
    pallas_call x1, Pallas kernels, block(): pl.pallas_call(functools.partial(kernel, nz, nx, factor), out_shape=(jax....  65.8 us
    pallas_call x1, Pallas kernels, add_branches(): pl.pallas_call(add_kernel, grid=(steps,), out_shape=(jax.ShapeDtypeStruct...  3.37 us

profile of v6, /device:TPU:1, one launch (start us, length us, event | category | flops | bytes accessed | tf_op | source)
XLA Modules:
  0.0 69.8 jit_solution(1133590607794610098)
XLA Ops:
  0.6 65.8 %window_block.1 = (bf16[16,32,1024]{2,1,0:T(8,128)(2,1)}, bf16[16,32,1024]{2,1,0:T(8,128)(2,1)}, f32[4,1536]{1,0:T(4,128)}, f32[4,512]{1,0:T(4,128)}, f32[1,4]{1,0:T(1,128)}) custom-call(bf16[16,32,1024]{2,1,0:T(8,128)(2,1)} %bitcast.8, bf16[16,32,1024]{2,1,0:T(8,128)(2,1)} %bitcast.10, f32[1,1024]{1,0:T(1,128)} %bitcast.13, bf16[1024,1536]{1,0:T(8,128)(2,1)} %wqkv_hbm.1, ...), custom_call_target="tpu_custom_call" | custom-call | tf_op jit(solution)/shard_map/window_block/pallas_call | solution.py:423
  66.4 3.4 %add_branches.1 = (bf16[16,32,1024]{2,1,0:T(8,128)(2,1)}, bf16[16,32,1024]{2,1,0:T(8,128)(2,1)}, f32[4,1536]{1,0:T(4,128)}, f32[4,512]{1,0:T(4,128)}, f32[1,4]{1,0:T(1,128)}) custom-call(bf16[16,32,1024]{2,1,0:T(8,128)(2,1)} %bitcast.9, bf16[16,32,1024]{2,1,0:T(8,128)(2,1)} %bitcast.11, bf16[16,32,1024]{2,1,0:T(8,128)(2,1)} %get-tuple-element.15.att_ref, ...), custom_call_target="tpu_custom_call" | custom-call | tf_op jit(solution)/shard_map/add_branches/pallas_call | solution.py:455
